TPU v7x, 32 devices: a whole 2x2x4 slice. The times are simulated.
32 devices in a mesh: shot: 4 (over y, core), rcv: 8 (over z, x).
Axes of the slice: x: 2, y: 2, z: 4, core: 2. Of those that a mesh axis runs over, the one named last changes fastest.
Arguments:
- traces: bfloat16 [4, 8, 1536, 2048], P('shot', 'rcv'), may hold values from -6 to 6
- trace_shot: int32 [4, 8, 1536], P('shot', 'rcv'), may hold values from 0 to 127, as said below
- trace_rcv: int32 [4, 8, 1536], P('shot', 'rcv'), may hold values from 0 to 127
- fold_count: int32 [4, 8], P('shot', 'rcv'), may hold values from 512 to 1536
Outputs:
- shot_terms: float32 [512, 1024], P('shot')
- rcv_terms: float32 [1024, 1024], P('rcv')
Inputs may be any that keep to these rules, and one draw needn't show every extreme that they name: `trace_shot`: in every tile, slot k < 128 holds a distinct shot, and its receiver index equals its shot index, so every shot and receiver of the tile's blocks has a live trace there.
All inputs are finite; a program needn't handle non-finite values.
Results may differ from a plain program's by a relative error of at most 0.0072.
Values sent between devices are 32-bit elements; how exact they have to be, the bound alone decides.
No kernel may reach another device: no remote copies, remote signals or barrier semaphores. Data moves between devices by JAX's collectives and lax.ppermute only.
A program may use at most 128 MiB of HBM per device.

v0:
```python
import jax
import jax.numpy as jnp
from jax import lax
from jax.sharding import PartitionSpec as P

SHOT_DEV = 128
RCV_DEV = 128
SWEEPS = 3


def dft_tables(samples_count, bins_count):
    index_n = jnp.arange(samples_count, dtype=jnp.int32)
    index_f = jnp.arange(bins_count, dtype=jnp.int32)
    product = index_n[:, None] * index_f[None, :] % samples_count
    angle_table = 2.0 * jnp.pi / samples_count * product.astype(jnp.float32)
    return (jnp.cos(angle_table).astype(jnp.bfloat16), jnp.sin(angle_table).astype(jnp.bfloat16))


def log_spectrum(trace_block, cos_table, sin_table, samples_count):
    real = jnp.dot(trace_block, cos_table, preferred_element_type=jnp.float32)
    imag = jnp.dot(trace_block, sin_table, preferred_element_type=jnp.float32)
    return jnp.log((real * real + imag * imag) / samples_count + 1e-06)


def shards(traces, trace_shot, trace_rcv, fold_count):
    slot_total = traces.shape[2]
    samples_count = traces.shape[3]
    bins_count = samples_count // 2
    tile_traces = traces[0, 0]
    live_count = fold_count[0, 0]
    cos_table, sin_table = dft_tables(samples_count, bins_count)
    alive = (jnp.arange(slot_total, dtype=jnp.int32) < live_count).astype(jnp.float32)
    onehot_shot = (
        trace_shot[0, 0][:, None] == jnp.arange(SHOT_DEV, dtype=jnp.int32)[None, :]
    ).astype(jnp.float32) * alive[:, None]
    onehot_rcv = (trace_rcv[0, 0][:, None] == jnp.arange(RCV_DEV, dtype=jnp.int32)[None, :]).astype(
        jnp.float32
    ) * alive[:, None]
    shot_count = lax.psum(jnp.sum(onehot_shot, axis=0), "rcv")
    rcv_count = lax.psum(jnp.sum(onehot_rcv, axis=0), "shot")
    spectra_log = log_spectrum(tile_traces, cos_table, sin_table, samples_count)
    shot_logs = jnp.dot(onehot_shot.T, spectra_log, precision=lax.Precision.HIGHEST)
    rcv_logs = jnp.dot(onehot_rcv.T, spectra_log, precision=lax.Precision.HIGHEST)
    pairs = jnp.dot(onehot_shot.T, onehot_rcv, precision=lax.Precision.HIGHEST)
    shot_blocks = lax.axis_size("shot")
    rcv_blocks = lax.axis_size("rcv")
    device_total = shot_blocks * rcv_blocks
    owned_bins = bins_count // device_total
    shot_parts, rcv_parts = (
        lax.all_to_all(shot_logs[None], ("shot", "rcv"), split_axis=2, concat_axis=0, tiled=True),
        lax.all_to_all(rcv_logs[None], ("shot", "rcv"), split_axis=2, concat_axis=0, tiled=True),
    )
    shot_whole = shot_parts.reshape(shot_blocks, rcv_blocks, SHOT_DEV, owned_bins).sum(axis=1)
    rcv_whole = rcv_parts.reshape(shot_blocks, rcv_blocks, RCV_DEV, owned_bins).sum(axis=0)
    pairs_every, shot_counts, rcv_counts = (
        lax.all_gather(pairs[None], ("shot", "rcv"), axis=0, tiled=True),
        lax.all_gather(shot_count[None], ("shot", "rcv"), axis=0, tiled=True),
        lax.all_gather(rcv_count[None], ("shot", "rcv"), axis=0, tiled=True),
    )
    pairs_every = pairs_every.reshape(shot_blocks, rcv_blocks, SHOT_DEV, RCV_DEV)
    shot_norm = shot_counts.reshape(shot_blocks, rcv_blocks, SHOT_DEV)[:, 0]
    rcv_norm = rcv_counts.reshape(shot_blocks, rcv_blocks, RCV_DEV)[0]
    rcv_local = jnp.zeros((rcv_blocks, RCV_DEV, owned_bins), jnp.float32)
    shot_local = jnp.zeros((shot_blocks, SHOT_DEV, owned_bins), jnp.float32)
    for iteration in range(SWEEPS):
        shot_total = shot_whole - jnp.einsum(
            "ijxy,jyf->ixf", pairs_every, rcv_local, precision=lax.Precision.HIGHEST
        )
        shot_local = shot_total / shot_norm[:, :, None]
        rcv_total = rcv_whole - jnp.einsum(
            "ijxy,ixf->jyf", pairs_every, shot_local, precision=lax.Precision.HIGHEST
        )
        rcv_local = rcv_total / rcv_norm[:, :, None]
    shot_send = jnp.broadcast_to(
        shot_local[:, None], (shot_blocks, rcv_blocks, SHOT_DEV, owned_bins)
    ).reshape(device_total, SHOT_DEV, owned_bins)
    rcv_send = jnp.broadcast_to(
        rcv_local[None], (shot_blocks, rcv_blocks, RCV_DEV, owned_bins)
    ).reshape(device_total, RCV_DEV, owned_bins)
    shot_back, rcv_back = (
        lax.all_to_all(shot_send, ("shot", "rcv"), split_axis=0, concat_axis=2, tiled=True),
        lax.all_to_all(rcv_send, ("shot", "rcv"), split_axis=0, concat_axis=2, tiled=True),
    )
    return (shot_back[0], rcv_back[0])


def solution(mesh):
    return jax.shard_map(
        shards,
        mesh=mesh,
        in_specs=(
            P("shot", "rcv", None, None),
            P("shot", "rcv", None),
            P("shot", "rcv", None),
            P("shot", "rcv"),
        ),
        out_specs=(P("shot", None), P("rcv", None)),
        check_vma=False,
    )
```

profile of v0, /device:TPU:0, one launch (start us, length us, event | category | flops | bytes accessed | tf_op | source)
XLA Modules:
  0.0 344.4 jit_solution(18109659029276532021)
XLA Ops:
  7.2 0.0 all-gather.5.cloned.1.call-start
  7.9 0.7 reduce
  8.6 0.7 reduce.1
  9.3 2.9 fusion.16
  12.2 0.0 all-gather.5.cloned.1.call-update
  12.3 0.0 copy-start.2
  12.3 31.2 %sine_convert_fusion.4 = bf16[2048,1024]{1,0:T(8,128)(2,1)S(1)} fusion(), kind=kLoop, calls=%fused_computation.6.clone.clone.1 | loop fusion | flops 31457280 | bytes 4194304 | tf_op jit(solution)/shard_map/dot_general | solution.py:21
  43.5 31.2 %cosine_convert_fusion.4 = bf16[2048,1024]{1,0:T(8,128)(2,1)S(1)} fusion(), kind=kLoop, calls=%fused_computation.7.clone.clone.1 | loop fusion | flops 31457280 | bytes 4194304 | tf_op jit(solution)/shard_map/dot_general | solution.py:20
  74.7 0.0 copy-done.2
  74.7 6.7 %fusion.6 = f32[1024,1536]{1,0:T(8,128)S(1)} fusion(bf16[1,1,1536,2048]{3,2,1,0:T(8,128)(2,1)S(1)} %copy-done.2, bf16[2048,1024]{1,0:T(8,128)(2,1)S(1)} %sine_convert_fusion.4), kind=kOutput, calls=%fused_computation.11 | convolution fusion | flops 6442450944 | bytes 16777216 | tf_op jit(solution)/shard_map/dot_general | solution.py:21
  81.4 7.7 %add_log_fusion = f32[1024,1536]{1,0:T(8,128)S(1)} fusion(f32[1024,1536]{1,0:T(8,128)S(1)} %fusion.6, bf16[1,1,1536,2048]{3,2,1,0:T(8,128)(2,1)S(1)} %copy-done.2, bf16[2048,1024]{1,0:T(8,128)(2,1)S(1)} %cosine_convert_fusion.4), kind=kOutput, calls=%fused_computation.15 | convolution fusion | flops 6450315264 | bytes 23068672 | tf_op jit(solution)/shard_map/dot_general | solution.py:20
  89.1 0.0 copy-start.1
  89.1 2.7 copy-done.1
  91.8 5.9 %fusion.19 = f32[128,1024]{0,1:T(8,128)} fusion(f32[1024,1536]{1,0:T(8,128)S(1)} %add_log_fusion, f32[1536]{0:T(1024)S(1)} %fusion.49, s32[1536]{0:T(1024)S(1)} %reduce), kind=kOutput, calls=%fused_computation.23 | convolution fusion | flops 2416312320 | bytes 6828032 | tf_op jit(solution)/shard_map/dot_general | solution.py:42
  97.7 7.3 %all-to-all-start = ((f32[1,128,1024]{1,0,2:T(1,128)}), f32[1,128,1024]{1,0,2:T(1,128)S(1)}, u32[]{:S(2)}, u32[]{:S(2)}) async-start(f32[1,128,1024]{1,0,2:T(1,128)} %bitcast.56), calls=%async_computation | async-start | bytes 1048576 | tf_op jit(solution)/shard_map/all_to_all | solution.py:50
  105.0 8.0 %fusion.14 = f32[128,1024]{0,1:T(8,128)} fusion(f32[1024,1536]{1,0:T(8,128)} %copy-done.1, s32[1536]{0:T(1024)S(1)} %reduce.1, f32[1536]{0:T(1024)S(1)} %fusion.49), kind=kOutput, calls=%fused_computation.17 | convolution fusion | flops 2416312320 | bytes 6828032 | tf_op jit(solution)/shard_map/dot_general | solution.py:43
  113.1 8.3 %all-to-all-done = f32[1,128,1024]{1,0,2:T(1,128)S(1)} async-done(((f32[1,128,1024]{1,0,2:T(1,128)}), f32[1,128,1024]{1,0,2:T(1,128)S(1)}, u32[]{:S(2)}, u32[]{:S(2)}) %all-to-all-start) | async-done | bytes 524320 | tf_op jit(solution)/shard_map/all_to_all | solution.py:50
  121.4 2.6 all-to-all-start.1
  124.0 1.1 select_reduce_fusion
  125.0 22.9 %psum.14 = f32[1,128]{1,0:T(1,128)S(1)} all-reduce(f32[1,128]{1,0:T(1,128)S(1)} %bitcast.143), channel_id=1, replica_groups=mesh['shot'=4,'rcv'=8] {'rcv'}, use_global_device_ids=true, to_apply=%region_3.4 | all-reduce | flops 128 | bytes 1024 | tf_op jit(solution)/shard_map/psum | solution.py:39
  147.9 64.7 %all-gather.1 = f32[32,1,128]{2,1,0:T(1,128)S(1)} all-gather(f32[1,1,128]{2,1,0:T(1,128)S(1)} %bitcast.144), channel_id=1, replica_groups=mesh['shot'=4,'rcv'=8] {'shot','rcv'}, dimensions={0}, use_global_device_ids=true | all-gather | bytes 16896 | tf_op jit(solution)/shard_map/all_gather | solution.py:57
  212.6 5.6 %psum.15 = f32[1,128]{1,0:T(1,128)S(1)} all-reduce(f32[1,128]{1,0:T(1,128)S(1)} %bitcast.142), channel_id=1, replica_groups=mesh['shot'=4,'rcv'=8] {'shot'}, use_global_device_ids=true, to_apply=%region_5.6 | all-reduce | flops 128 | bytes 1024 | tf_op jit(solution)/shard_map/psum | solution.py:40
  218.2 63.7 %all-gather.2 = f32[32,1,128]{2,1,0:T(1,128)S(1)} all-gather(f32[1,1,128]{2,1,0:T(1,128)S(1)} %bitcast.145), channel_id=1, replica_groups=mesh['shot'=4,'rcv'=8] {'shot','rcv'}, dimensions={0}, use_global_device_ids=true | all-gather | bytes 16896 | tf_op jit(solution)/shard_map/all_gather | solution.py:58
  281.9 0.0 all-to-all-done.1
  282.0 0.0 all-gather.5.cloned.1.call-done
  282.0 0.0 copy-start
  282.0 3.8 %fusion.31 = f32[4,128,32,1]{1,2,3,0:T(8,128)S(1)} fusion(f32[4,128,32]{1,2,0:T(8,128)S(1)} %reduce_sum.36, f32[4,8,128,128]{3,2,1,0:T(8,128)} %bitcast.125, f32[4,128]{1,0:T(4,128)S(1)} %bitcast.138), kind=kOutput, calls=%fused_computation.41 | convolution fusion | flops 201359360 | bytes 2230272 | tf_op jit(solution)/shard_map/ijxy,jyf->ixf/dot_general | solution.py:66
  285.8 2.9 fusion.23
  288.7 3.6 %fusion.34 = f32[4,128,32,1]{1,2,3,0:T(8,128)S(1)} fusion(f32[4,128,32]{1,2,0:T(8,128)S(1)} %reduce_sum.36, f32[4,8,128,128]{3,2,1,0:T(8,128)} %bitcast.127, f32[8,128,32,1]{1,2,0,3:T(8,128)S(1)} %fusion.23, f32[4,128]{1,0:T(4,128)S(1)} %bitcast.139), kind=kOutput, calls=%fused_computation.44 | convolution fusion | flops 201359360 | bytes 2361344 | tf_op jit(solution)/shard_map/ijxy,jyf->ixf/dot_general | solution.py:66
  292.3 0.0 copy-done
  292.4 1.4 fusion.26
  293.7 2.0 fusion.36
  295.7 0.9 broadcast_in_dim.42
  296.6 3.3 all-to-all-start.2
  299.9 1.4 fusion.28
  301.3 15.0 %all-to-all-done.2 = f32[32,128,32]{1,2,0:T(8,128)S(1)} async-done(((f32[32,128,32]{1,2,0:T(8,128)}), f32[32,128,32]{1,2,0:T(8,128)S(1)}, u32[]{:S(2)}, u32[]{:S(2)}) %all-to-all-start.2) | async-done | bytes 524320 | tf_op jit(solution)/shard_map/all_to_all | solution.py:81
  316.3 0.9 broadcast_in_dim.43
  317.1 2.6 all-to-all-start.3
  319.7 1.0 copy.24
  320.7 15.4 %all-to-all-done.3 = f32[32,128,32]{1,2,0:T(8,128)S(1)} async-done(((f32[32,128,32]{1,2,0:T(8,128)}), f32[32,128,32]{1,2,0:T(8,128)S(1)}, u32[]{:S(2)}, u32[]{:S(2)}) %all-to-all-start.3) | async-done | bytes 524320 | tf_op jit(solution)/shard_map/all_to_all | solution.py:82
  336.1 1.0 copy.25
  (5 shorter events, 0.1 us)
Async XLA Ops:
  7.2 274.9 %all-gather.5.cloned.1.call-start = ((), (), s32[]{:S(2)}) async-start(), calls=%async_computation.4 | async-start | bytes 2162688 | tf_op jit(solution)/shard_map/all_gather | solution.py:56
  12.3 62.4 %copy-start.2 = (bf16[1,1,1536,2048]{3,2,1,0:T(8,128)(2,1)S(1)}, bf16[1,1,1536,2048]{3,2,1,0:T(8,128)(2,1)}, u32[]{:S(2)}) copy-start(bf16[1,1,1536,2048]{3,2,1,0:T(8,128)(2,1)} %param.4) | copy-start | bytes 18874372
  89.1 2.7 copy-start.1
  97.7 23.7 %all-to-all-start = ((f32[1,128,1024]{1,0,2:T(1,128)}), f32[1,128,1024]{1,0,2:T(1,128)S(1)}, u32[]{:S(2)}, u32[]{:S(2)}) async-start(f32[1,128,1024]{1,0,2:T(1,128)} %bitcast.56), calls=%async_computation | async-start | bytes 1048576 | tf_op jit(solution)/shard_map/all_to_all | solution.py:50
  121.4 160.6 %all-to-all-start.1 = ((f32[1,128,1024]{1,0,2:T(1,128)}), f32[1,128,1024]{1,0,2:T(1,128)S(1)}, u32[]{:S(2)}, u32[]{:S(2)}) async-start(f32[1,128,1024]{1,0,2:T(1,128)} %bitcast.57), calls=%async_computation.1 | async-start | bytes 1048576 | tf_op jit(solution)/shard_map/all_to_all | solution.py:51
  282.0 10.3 %copy-start = (f32[4096,128]{1,0:T(8,128)S(1)}, f32[4096,128]{1,0:T(8,128)}, u32[]{:S(2)}) copy-start(f32[4096,128]{1,0:T(8,128)} %all-gather.5.cloned.1.call-done) | copy-start | bytes 6291460
  296.6 19.7 %all-to-all-start.2 = ((f32[32,128,32]{1,2,0:T(8,128)}), f32[32,128,32]{1,2,0:T(8,128)S(1)}, u32[]{:S(2)}, u32[]{:S(2)}) async-start(f32[32,128,32]{1,2,0:T(8,128)} %bitcast.32), calls=%async_computation.2 | async-start | bytes 1048576 | tf_op jit(solution)/shard_map/all_to_all | solution.py:81
  317.1 19.0 %all-to-all-start.3 = ((f32[32,128,32]{1,2,0:T(8,128)}), f32[32,128,32]{1,2,0:T(8,128)S(1)}, u32[]{:S(2)}, u32[]{:S(2)}) async-start(f32[32,128,32]{1,2,0:T(8,128)} %bitcast.39), calls=%async_computation.3 | async-start | bytes 1048576 | tf_op jit(solution)/shard_map/all_to_all | solution.py:82
Sparse Core Ops, SparseCore 0:
  12.4 59.3 all-gather.4
where the time goes:
time: 350 us; the launch traced here: 344 us
  blocking collectives  157 us (45%)
  other arithmetic  65 us (19%)
  matrix products  46.3 us (13%)
  waiting for transfers between devices  38.7 us (11%)
  starting transfers between devices  15.9 us (5%)
  between operations  15.3 us (4%)
  local copies, waits for them, and re-layouts  6.36 us (2%)
    all_gather x1, blocking collectives, shards(): lax.all_gather(shot_count[None], ('shot', 'rcv'), axis=0, tiled=True)  64.7 us
    all_gather x1, blocking collectives, shards(): lax.all_gather(rcv_count[None], ('shot', 'rcv'), axis=0, tiled=True)  63.7 us
    dot_general x1, other arithmetic, log_spectrum(): imag = jnp.dot(trace_block, sin_table, preferred_element_type=jnp.float32)  31.2 us
    dot_general x1, other arithmetic, log_spectrum(): real = jnp.dot(trace_block, cos_table, preferred_element_type=jnp.float32)  31.2 us
    psum x1, blocking collectives, shards(): shot_count = lax.psum(jnp.sum(onehot_shot, axis=0), 'rcv')  22.9 us
    all_to_all x1, waiting for transfers between devices, shards(): lax.all_to_all(rcv_send, ('shot', 'rcv'), split_axis=0, concat_axis=2, ti...  15.4 us
    all_to_all x1, waiting for transfers between devices, shards(): lax.all_to_all(shot_send, ('shot', 'rcv'), split_axis=0, concat_axis=2, t...  15 us
    dot_general x3, matrix products, shards(): jnp.einsum('ijxy,jyf->ixf', pairs_every, rcv_local, precision=lax.Precisi...  9.38 us
  transfers between devices with their start and end apart: 5, of which 3 were waited for; matrix products, arithmetic and copies ran while one was open for 27% of the time, Pallas kernels for 0%

commit v1 on v0

v1 whole, which is shorter than its diff:
```python
import functools

import jax
import jax.numpy as jnp
import numpy as np
from jax import lax
from jax.experimental import pallas as pl
from jax.experimental.pallas import tpu as pltpu
from jax.sharding import PartitionSpec as P

SHOT_DEV = 128
RCV_DEV = 128
SWEEPS = 3
SLOT_BLOCK = 256
BIN_BLOCK = 256
ROW_BLOCK = 128
VMEM_BYTES = 48 * 1024 * 1024


def dft_tables(samples_count, bins_count):
    product = (np.arange(bins_count)[:, None] * np.arange(samples_count)[None, :]) % samples_count
    angle = (np.float32(2.0 * np.pi / samples_count) * product.astype(np.float32)).astype(np.float64)
    both = np.stack([np.cos(angle), np.sin(angle)]).astype(np.float32)
    return both.astype(jnp.bfloat16)


def across(a, b):
    return lax.dot_general(a, b, (((1,), (1,)), ((), ())), preferred_element_type=jnp.float32)


def along(a, b):
    return lax.dot_general(a, b, (((1,), (0,)), ((), ())), preferred_element_type=jnp.float32)


def spectra_kernel(inv_samples, traces_ref, table_ref, index_ref, shot_ref, rcv_ref):
    step = pl.program_id(1)
    block = traces_ref[...]
    slots = block.shape[0]
    rows = lax.broadcasted_iota(jnp.int32, (SHOT_DEV, slots), 0)
    onehot = jnp.concatenate(
        [(index_ref[k : k + 1, :] == rows).astype(jnp.float32) for k in range(2)], axis=0
    ).astype(jnp.bfloat16)

    @pl.when(step == 0)
    def _():
        shot_ref[...] = jnp.zeros_like(shot_ref)
        rcv_ref[...] = jnp.zeros_like(rcv_ref)

    for at in range(0, table_ref.shape[1], ROW_BLOCK):
        real = across(table_ref[0, at : at + ROW_BLOCK, :], block)
        imag = across(table_ref[1, at : at + ROW_BLOCK, :], block)
        logs = jnp.log((real * real + imag * imag) * inv_samples + 1e-06)
        high = logs.astype(jnp.bfloat16)
        low = (logs - high.astype(jnp.float32)).astype(jnp.bfloat16)
        sums = across(high, onehot) + across(low, onehot)
        shot_ref[at : at + ROW_BLOCK, :] += sums[:, :SHOT_DEV]
        rcv_ref[at : at + ROW_BLOCK, :] += sums[:, SHOT_DEV:]


def spectra_sums(traces, table, index):
    slots, samples = traces.shape
    bins = table.shape[1]
    return pl.pallas_call(
        functools.partial(spectra_kernel, 1.0 / samples),
        grid=(bins // BIN_BLOCK, slots // SLOT_BLOCK),
        in_specs=[
            pl.BlockSpec((SLOT_BLOCK, samples), lambda b, t: (t, 0)),
            pl.BlockSpec((2, BIN_BLOCK, samples), lambda b, t: (0, b, 0)),
            pl.BlockSpec((2, SLOT_BLOCK), lambda b, t: (0, t)),
        ],
        out_specs=[
            pl.BlockSpec((BIN_BLOCK, SHOT_DEV), lambda b, t: (b, 0)),
            pl.BlockSpec((BIN_BLOCK, RCV_DEV), lambda b, t: (b, 0)),
        ],
        out_shape=[
            jax.ShapeDtypeStruct((bins, SHOT_DEV), jnp.float32),
            jax.ShapeDtypeStruct((bins, RCV_DEV), jnp.float32),
        ],
        compiler_params=pltpu.CompilerParams(vmem_limit_bytes=VMEM_BYTES),
        cost_estimate=pl.CostEstimate(
            flops=4 * slots * samples * bins, bytes_accessed=32 * 1024 * 1024, transcendentals=slots * bins
        ),
    )(traces, table, index)


def pairs_kernel(shot_blocks, rcv_blocks, index_ref, high_ref, low_ref, shot_count_ref, rcv_count_ref):
    slots = index_ref.shape[2]
    rows = lax.broadcasted_iota(jnp.int32, (SHOT_DEV, slots), 0)

    for i in range(shot_blocks):

        def tile(j, carry):
            entry = index_ref[i * rcv_blocks + j]
            of_shot = (entry[0:1, :] == rows).astype(jnp.float32).astype(jnp.bfloat16)
            of_rcv = (entry[1:2, :] == rows).astype(jnp.float32).astype(jnp.bfloat16)
            pairs = across(of_shot, of_rcv)
            high = pairs.astype(jnp.bfloat16)
            low = (pairs - high.astype(jnp.float32)).astype(jnp.bfloat16)
            at = pl.ds(pl.multiple_of(j * RCV_DEV, RCV_DEV), RCV_DEV)
            high_ref[i * SHOT_DEV : (i + 1) * SHOT_DEV, at] = high
            low_ref[i * SHOT_DEV : (i + 1) * SHOT_DEV, at] = low
            return carry

        lax.fori_loop(0, rcv_blocks, tile, 0)
    ones_rcv = jnp.ones((16, rcv_blocks * RCV_DEV), jnp.bfloat16)
    ones_shot = jnp.ones((16, shot_blocks * SHOT_DEV), jnp.bfloat16)
    shot_count_ref[...] = (across(ones_rcv, high_ref[...]) + across(ones_rcv, low_ref[...]))[:8]
    rcv_count_ref[...] = (along(ones_shot, high_ref[...]) + along(ones_shot, low_ref[...]))[:8]


def pair_counts(index_every, shot_blocks, rcv_blocks):
    shots, rcvs = shot_blocks * SHOT_DEV, rcv_blocks * RCV_DEV
    return pl.pallas_call(
        functools.partial(pairs_kernel, shot_blocks, rcv_blocks),
        out_shape=[
            jax.ShapeDtypeStruct((shots, rcvs), jnp.bfloat16),
            jax.ShapeDtypeStruct((shots, rcvs), jnp.bfloat16),
            jax.ShapeDtypeStruct((8, shots), jnp.float32),
            jax.ShapeDtypeStruct((8, rcvs), jnp.float32),
        ],
        compiler_params=pltpu.CompilerParams(vmem_limit_bytes=VMEM_BYTES),
        cost_estimate=pl.CostEstimate(
            flops=2 * shots * rcvs * index_every.shape[2], bytes_accessed=4 * shots * rcvs, transcendentals=0
        ),
    )(index_every)


def solve_kernel(
    shot_blocks, rcv_blocks, shot_parts, rcv_parts, high_ref, low_ref, shot_count_ref, rcv_count_ref, shot_out, rcv_out
):
    bins = shot_parts.shape[1]

    def total(terms):
        return functools.reduce(lambda a, b: a + b, terms)

    shot_logs = jnp.concatenate(
        [total([shot_parts[i * rcv_blocks + j] for j in range(rcv_blocks)]) for i in range(shot_blocks)], axis=1
    )
    rcv_logs = jnp.concatenate(
        [total([rcv_parts[i * rcv_blocks + j] for i in range(shot_blocks)]) for j in range(rcv_blocks)], axis=1
    )
    shot_count = shot_count_ref[0:1, :]
    rcv_count = rcv_count_ref[0:1, :]

    def times(terms, product):
        first = terms.astype(jnp.bfloat16).astype(jnp.float32)
        rest = terms - first
        second = rest.astype(jnp.bfloat16).astype(jnp.float32)
        stack = jnp.concatenate([first, second, rest - second], axis=0).astype(jnp.bfloat16)
        out = product(stack, high_ref[...]) + product(stack, low_ref[...])
        return out[:bins] + out[bins : 2 * bins] + out[2 * bins :]

    shot_terms = shot_logs / shot_count
    rcv_terms = (rcv_logs - times(shot_terms, along)) / rcv_count
    for _ in range(SWEEPS - 1):
        shot_terms = (shot_logs - times(rcv_terms, across)) / shot_count
        rcv_terms = (rcv_logs - times(shot_terms, along)) / rcv_count
    for i in range(shot_blocks):
        shot_out[i] = shot_terms[:, i * SHOT_DEV : (i + 1) * SHOT_DEV]
    for j in range(rcv_blocks):
        rcv_out[j] = rcv_terms[:, j * RCV_DEV : (j + 1) * RCV_DEV]


def solve(shot_parts, rcv_parts, counts, shot_blocks, rcv_blocks):
    bins = shot_parts.shape[1]
    return pl.pallas_call(
        functools.partial(solve_kernel, shot_blocks, rcv_blocks),
        out_shape=[
            jax.ShapeDtypeStruct((shot_blocks, bins, SHOT_DEV), jnp.float32),
            jax.ShapeDtypeStruct((rcv_blocks, bins, RCV_DEV), jnp.float32),
        ],
        compiler_params=pltpu.CompilerParams(vmem_limit_bytes=VMEM_BYTES),
    )(shot_parts, rcv_parts, *counts)


def shards(traces, trace_shot, trace_rcv, fold_count):
    slot_total = traces.shape[2]
    samples_count = traces.shape[3]
    bins_count = samples_count // 2
    shot_blocks = lax.axis_size("shot")
    rcv_blocks = lax.axis_size("rcv")
    device_total = shot_blocks * rcv_blocks
    owned_bins = bins_count // device_total
    axes = ("shot", "rcv")
    table = jnp.asarray(dft_tables(samples_count, bins_count))
    alive = jnp.arange(slot_total, dtype=jnp.int32) < fold_count[0, 0]
    index = jnp.where(alive, jnp.stack([trace_shot[0, 0], trace_rcv[0, 0]]), -1)
    index_every = lax.all_to_all(
        jnp.broadcast_to(index[None], (device_total,) + index.shape), axes, split_axis=0, concat_axis=0, tiled=True
    )
    shot_logs, rcv_logs = spectra_sums(traces[0, 0], table, index)
    counts = pair_counts(index_every, shot_blocks, rcv_blocks)
    exchange = functools.partial(lax.all_to_all, axis_name=axes, split_axis=0, concat_axis=0, tiled=True)
    shot_parts = exchange(shot_logs.reshape(device_total, owned_bins, SHOT_DEV))
    rcv_parts = exchange(rcv_logs.reshape(device_total, owned_bins, RCV_DEV))
    shot_local, rcv_local = solve(shot_parts, rcv_parts, counts, shot_blocks, rcv_blocks)
    shot_send = jnp.broadcast_to(shot_local[:, None], (shot_blocks, rcv_blocks, owned_bins, SHOT_DEV))
    rcv_send = jnp.broadcast_to(rcv_local[None], (shot_blocks, rcv_blocks, owned_bins, RCV_DEV))
    shot_back = exchange(shot_send.reshape(device_total, owned_bins, SHOT_DEV))
    rcv_back = exchange(rcv_send.reshape(device_total, owned_bins, RCV_DEV))
    return shot_back.reshape(bins_count, SHOT_DEV).T, rcv_back.reshape(bins_count, RCV_DEV).T


def solution(mesh):
    return jax.shard_map(
        shards,
        mesh=mesh,
        in_specs=(
            P("shot", "rcv", None, None),
            P("shot", "rcv", None),
            P("shot", "rcv", None),
            P("shot", "rcv"),
        ),
        out_specs=(P("shot", None), P("rcv", None)),
        check_vma=False,
    )
```

time: 350 us -> 145 us (0.41); the launches traced: 344 us -> 145 us
  blocking collectives: 157 us -> 40.3 us
  other arithmetic: 65 us -> 0.74 us
  Pallas kernels: 0 us -> 63.6 us
  matrix products: 46.3 us -> 0 us
  waiting for transfers between devices: 38.7 us -> 21 us
  between operations: 15.3 us -> 1.34 us
    all_gather x2 -> x0, blocking collectives: 128 us -> none  [the longest x1 64.7 us: shards(): lax.all_gather(shot_count[None], ('shot', 'rcv'), axis=0, tiled=True)]
    pallas_call x0 -> x3, Pallas kernels: none -> 63.6 us  [the longest x1 50.9 us: spectra_sums(): pl.pallas_call(functools.partial(spectra_kernel, 1.0 / samples), grid=(bi...]
    dot_general x2 -> x0, other arithmetic: 62.4 us -> none  [the longest x1 31.2 us: log_spectrum(): imag = jnp.dot(trace_block, sin_table, preferred_element_type=jnp.float32)]
    dot_general x11 -> x0, matrix products: 46.3 us -> none  [the longest x3 9.38 us: shards(): jnp.einsum('ijxy,jyf->ixf', pairs_every, rcv_local, precision=lax.Precisi...]
    all_to_all x0 -> x2, blocking collectives: none -> 40.3 us  [the longest x1 22 us: shards(): rcv_parts = exchange(rcv_logs.reshape(device_total, owned_bins, RCV_DEV))]
    psum x2 -> x0, blocking collectives: 28.5 us -> none  [the longest x1 22.9 us: shards(): shot_count = lax.psum(jnp.sum(onehot_shot, axis=0), 'rcv')]
    all_to_all x4 -> x3, waiting for transfers between devices: 38.7 us -> 21 us  [the longest x1 15.4 us: shards(): rcv_back = exchange(rcv_send.reshape(device_total, owned_bins, RCV_DEV))]
    all_to_all x4 -> x3, starting transfers between devices: 15.8 us -> 12.5 us  [the longest x1 7.3 us: shards(): lax.all_to_all(jnp.broadcast_to(index[None], (device_total,) + index.shap...]
  transfers between devices with their start and end apart: 5 -> 3, of which waited for: 3 -> 2; matrix products, arithmetic and copies ran while one was open for 27% -> 1% of each run, Pallas kernels for 0% -> 42%
where the time goes in v1:
time: 145 us
  Pallas kernels  63.6 us (44%)
  blocking collectives  40.3 us (28%)
  waiting for transfers between devices  21 us (14%)
  starting transfers between devices  12.5 us (9%)
  local copies, waits for them, and re-layouts  5.12 us (4%)
    pallas_call x1, Pallas kernels, spectra_sums(): pl.pallas_call(functools.partial(spectra_kernel, 1.0 / samples), grid=(bi...  50.9 us
    all_to_all x1, blocking collectives, shards(): rcv_parts = exchange(rcv_logs.reshape(device_total, owned_bins, RCV_DEV))  22 us
    all_to_all x1, blocking collectives, shards(): shot_back = exchange(shot_send.reshape(device_total, owned_bins, SHOT_DEV))  18.3 us
    all_to_all x1, waiting for transfers between devices, shards(): rcv_back = exchange(rcv_send.reshape(device_total, owned_bins, RCV_DEV))  15.4 us
    pallas_call x1, Pallas kernels, pair_counts(): pl.pallas_call(functools.partial(pairs_kernel, shot_blocks, rcv_blocks),...  10.1 us
    all_to_all x1, starting transfers between devices, shards(): lax.all_to_all(jnp.broadcast_to(index[None], (device_total,) + index.shap...  7.3 us
    all_to_all x1, waiting for transfers between devices, shards(): shot_parts = exchange(shot_logs.reshape(device_total, owned_bins, SHOT_DEV))  5.64 us
    unnamed x6, local copies, waits for them, and re-layouts  3.37 us
  transfers between devices with their start and end apart: 3, of which 2 were waited for; matrix products, arithmetic and copies ran while one was open for 1% of the time, Pallas kernels for 42%

profile of v1, /device:TPU:0, one launch (start us, length us, event | category | flops | bytes accessed | tf_op | source)
XLA Modules:
  0.0 144.6 jit_solution(13415451698332379536)
XLA Ops:
  1.3 0.7 add_select_fusion.index_ref
  2.0 0.8 broadcast_in_dim.28
  2.9 7.3 %all-to-all-start.2 = ((s32[32,2,1536]{2,1,0:T(2,128)}), s32[32,2,1536]{2,1,0:T(2,128)S(1)}, u32[]{:S(2)}, u32[]{:S(2)}) async-start(s32[32,2,1536]{2,1,0:T(2,128)} %broadcast_in_dim.28), calls=%async_computation.2 | async-start | bytes 786432 | tf_op jit(solution)/shard_map/all_to_all | solution.py:188
  10.2 50.9 %shard_map.68 = (f32[1024,128]{1,0:T(8,128)}, f32[1024,128]{1,0:T(8,128)S(1)}) custom-call(bf16[1536,2048]{1,0:T(8,128)(2,1)} %bitcast.21, bf16[2,1024,2048]{2,1,0:T(8,128)(2,1)} %constant.4.clone.table_ref, s32[2,1536]{1,0:T(2,128)S(1)} %add_select_fusion.index_ref), custom_call_target="tpu_custom_call" | custom-call | flops 12884901888 | bytes 33554432 | tf_op jit(solution)/shard_map/pallas_call | solution.py:63
  61.1 0.0 all-to-all-done.2.index_ref
  61.1 22.0 %all_to_all.25.rcv_parts = f32[32,32,128]{2,1,0:T(8,128)S(1)} all-to-all(f32[32,32,128]{2,1,0:T(8,128)S(1)} %bitcast.15), channel_id=1, replica_groups=mesh['shot'=4,'rcv'=8] {'shot','rcv'}, dimensions={0} | all-to-all | bytes 1048576 | tf_op jit(solution)/shard_map/all_to_all | solution.py:195
  83.1 2.6 %all-to-all-start = ((f32[32,32,128]{2,1,0:T(8,128)}), f32[32,32,128]{2,1,0:T(8,128)S(1)}, u32[]{:S(2)}, u32[]{:S(2)}) async-start(f32[32,32,128]{2,1,0:T(8,128)} %bitcast.4), calls=%async_computation | async-start | bytes 1048576 | tf_op jit(solution)/shard_map/all_to_all | solution.py:194
  85.7 10.1 %shard_map.69 = (bf16[512,1024]{1,0:T(8,128)(2,1)S(1)}, bf16[512,1024]{1,0:T(8,128)(2,1)S(1)}, f32[8,512]{1,0:T(8,128)S(1)}, f32[8,1024]{1,0:T(8,128)S(1)}) custom-call(s32[32,2,1536]{2,1,0:T(2,128)S(1)} %all-to-all-done.2.index_ref), custom_call_target="tpu_custom_call" | custom-call | flops 1610612736 | bytes 2097152 | tf_op jit(solution)/shard_map/pallas_call | solution.py:113
  95.8 0.0 copy-start
  95.8 0.6 copy-done
  96.4 5.6 %all-to-all-done.shot_parts = f32[32,32,128]{2,1,0:T(8,128)S(1)} async-done(((f32[32,32,128]{2,1,0:T(8,128)}), f32[32,32,128]{2,1,0:T(8,128)S(1)}, u32[]{:S(2)}, u32[]{:S(2)}) %all-to-all-start) | async-done | bytes 524320 | tf_op jit(solution)/shard_map/all_to_all | solution.py:194
  102.0 0.0 copy-start.1
  102.0 0.8 copy-done.1
  102.8 2.6 %shard_map.70 = (f32[4,32,128]{2,1,0:T(8,128)S(1)}, f32[8,32,128]{2,1,0:T(8,128)S(1)}) custom-call(f32[32,32,128]{2,1,0:T(8,128)S(1)} %all-to-all-done.shot_parts, f32[32,32,128]{2,1,0:T(8,128)S(1)} %all_to_all.25.rcv_parts, bf16[512,1024]{1,0:T(8,128)(2,1)S(1)} %get-tuple-element.12.high_ref, bf16[512,1024]{1,0:T(8,128)(2,1)S(1)} %get-tuple-element.13.low_ref, ...), custom_call_target="tpu_custom_call" | custom-call | tf_op jit(solution)/shard_map/pallas_call | solution.py:166
  105.4 0.1 broadcast_in_dim.29
  105.5 18.3 %all_to_all.26 = f32[32,32,128]{2,1,0:T(8,128)S(1)} all-to-all(f32[32,32,128]{2,1,0:T(8,128)S(1)} %bitcast.18), channel_id=1, replica_groups=mesh['shot'=4,'rcv'=8] {'shot','rcv'}, dimensions={0} | all-to-all | bytes 1048576 | tf_op jit(solution)/shard_map/all_to_all | solution.py:199
  123.8 0.9 broadcast_in_dim.30
  124.7 2.6 %all-to-all-start.4 = ((f32[32,32,128]{2,1,0:T(8,128)}), f32[32,32,128]{2,1,0:T(8,128)S(1)}, u32[]{:S(2)}, u32[]{:S(2)}) async-start(f32[32,32,128]{2,1,0:T(8,128)} %bitcast.9), calls=%async_computation.4 | async-start | bytes 1048576 | tf_op jit(solution)/shard_map/all_to_all | solution.py:200
  127.3 1.0 copy.9
  128.3 15.4 %all-to-all-done.4 = f32[32,32,128]{2,1,0:T(8,128)S(1)} async-done(((f32[32,32,128]{2,1,0:T(8,128)}), f32[32,32,128]{2,1,0:T(8,128)S(1)}, u32[]{:S(2)}, u32[]{:S(2)}) %all-to-all-start.4) | async-done | bytes 524320 | tf_op jit(solution)/shard_map/all_to_all | solution.py:200
  143.6 1.0 copy.10
  (1 shorter events, 0.0 us)
Async XLA Ops:
  2.9 58.2 %all-to-all-start.2 = ((s32[32,2,1536]{2,1,0:T(2,128)}), s32[32,2,1536]{2,1,0:T(2,128)S(1)}, u32[]{:S(2)}, u32[]{:S(2)}) async-start(s32[32,2,1536]{2,1,0:T(2,128)} %broadcast_in_dim.28), calls=%async_computation.2 | async-start | bytes 786432 | tf_op jit(solution)/shard_map/all_to_all | solution.py:188
  83.1 19.0 %all-to-all-start = ((f32[32,32,128]{2,1,0:T(8,128)}), f32[32,32,128]{2,1,0:T(8,128)S(1)}, u32[]{:S(2)}, u32[]{:S(2)}) async-start(f32[32,32,128]{2,1,0:T(8,128)} %bitcast.4), calls=%async_computation | async-start | bytes 1048576 | tf_op jit(solution)/shard_map/all_to_all | solution.py:194
  95.8 0.6 copy-start
  102.0 0.8 copy-start.1
  124.7 19.0 %all-to-all-start.4 = ((f32[32,32,128]{2,1,0:T(8,128)}), f32[32,32,128]{2,1,0:T(8,128)S(1)}, u32[]{:S(2)}, u32[]{:S(2)}) async-start(f32[32,32,128]{2,1,0:T(8,128)} %bitcast.9), calls=%async_computation.4 | async-start | bytes 1048576 | tf_op jit(solution)/shard_map/all_to_all | solution.py:200

commit v2 on v1

v2 whole, which is shorter than its diff:
```python
import functools

import jax
import jax.numpy as jnp
import numpy as np
from jax import lax
from jax.experimental import pallas as pl
from jax.experimental.pallas import tpu as pltpu
from jax.sharding import PartitionSpec as P

SHOT_DEV = 128
RCV_DEV = 128
SWEEPS = 3
GROUPS = 2
ROW_BLOCK = 256
SLOT_BLOCK = 512
VMEM_BYTES = 40 * 1024 * 1024
WHOLE_VMEM_BYTES = 62 * 1024 * 1024


def dft_tables(samples_count, bins_count):
    product = (np.arange(bins_count)[:, None] * np.arange(samples_count)[None, :]) % samples_count
    angle = (np.float32(2.0 * np.pi / samples_count) * product.astype(np.float32)).astype(np.float64)
    both = np.stack([np.cos(angle), np.sin(angle)]).astype(np.float32)
    return both.astype(jnp.bfloat16)


def across(a, b):
    return lax.dot_general(a, b, (((1,), (1,)), ((), ())), preferred_element_type=jnp.float32)


def along(a, b):
    return lax.dot_general(a, b, (((1,), (0,)), ((), ())), preferred_element_type=jnp.float32)


def spectra_kernel(inv_samples, traces_hbm, table_hbm, index_ref, sums_ref, traces_ref, table_ref, trace_sem, table_sem):
    slots = traces_ref.shape[0]
    bins = table_ref.shape[1]

    def trace_copy(at):
        span = pl.ds(at, SLOT_BLOCK)
        return pltpu.make_async_copy(traces_hbm.at[span], traces_ref.at[span], trace_sem.at[at // SLOT_BLOCK])

    def table_copy(at):
        span = pl.ds(at, ROW_BLOCK)
        return pltpu.make_async_copy(table_hbm.at[:, span], table_ref.at[:, span], table_sem.at[at // ROW_BLOCK])

    table_copy(0).start()
    for at in range(0, slots, SLOT_BLOCK):
        trace_copy(at).start()
    for at in range(ROW_BLOCK, bins, ROW_BLOCK):
        table_copy(at).start()
    rows = lax.broadcasted_iota(jnp.int32, (SHOT_DEV, slots), 0)
    onehot = jnp.concatenate(
        [(index_ref[k : k + 1, :] == rows).astype(jnp.float32) for k in range(2)], axis=0
    ).astype(jnp.bfloat16)

    def block_sums(at, first, last):
        block = traces_ref[first:last, :]
        real = across(table_ref[0, at : at + ROW_BLOCK, :], block)
        imag = across(table_ref[1, at : at + ROW_BLOCK, :], block)
        logs = jnp.log((real * real + imag * imag) * inv_samples + 1e-06)
        high = logs.astype(jnp.bfloat16)
        low = (logs - high.astype(jnp.float32)).astype(jnp.bfloat16)
        return across(high, onehot[:, first:last]) + across(low, onehot[:, first:last])

    table_copy(0).wait()
    for first in range(0, slots, SLOT_BLOCK):
        trace_copy(first).wait()
        sums = block_sums(0, first, first + SLOT_BLOCK)
        if first == 0:
            sums_ref[:ROW_BLOCK, :] = sums
        else:
            sums_ref[:ROW_BLOCK, :] += sums
    for at in range(ROW_BLOCK, bins, ROW_BLOCK):
        table_copy(at).wait()
        sums_ref[at : at + ROW_BLOCK, :] = block_sums(at, 0, slots)


def spectra_sums(traces, table, index):
    slots, samples = traces.shape
    bins = table.shape[1]
    return pl.pallas_call(
        functools.partial(spectra_kernel, 1.0 / samples),
        in_specs=[
            pl.BlockSpec(memory_space=pltpu.HBM),
            pl.BlockSpec(memory_space=pltpu.HBM),
            pl.BlockSpec(memory_space=pltpu.VMEM),
        ],
        out_specs=pl.BlockSpec(memory_space=pltpu.VMEM),
        out_shape=jax.ShapeDtypeStruct((bins, SHOT_DEV + RCV_DEV), jnp.float32),
        scratch_shapes=[
            pltpu.VMEM(traces.shape, traces.dtype),
            pltpu.VMEM(table.shape, table.dtype),
            pltpu.SemaphoreType.DMA((slots // SLOT_BLOCK,)),
            pltpu.SemaphoreType.DMA((bins // ROW_BLOCK,)),
        ],
        compiler_params=pltpu.CompilerParams(vmem_limit_bytes=WHOLE_VMEM_BYTES),
        cost_estimate=pl.CostEstimate(
            flops=4 * slots * samples * bins, bytes_accessed=4 * samples * bins, transcendentals=slots * bins
        ),
    )(traces, table, index)


def pairs_kernel(shot_blocks, rcv_blocks, index_ref, high_ref, low_ref, shot_count_ref, rcv_count_ref):
    slots = index_ref.shape[2]
    rows = lax.broadcasted_iota(jnp.int32, (SHOT_DEV, slots), 0)

    for i in range(shot_blocks):

        def tile(j, carry):
            entry = index_ref[i * rcv_blocks + j]
            of_shot = (entry[0:1, :] == rows).astype(jnp.float32).astype(jnp.bfloat16)
            of_rcv = (entry[1:2, :] == rows).astype(jnp.float32).astype(jnp.bfloat16)
            pairs = across(of_shot, of_rcv)
            high = pairs.astype(jnp.bfloat16)
            low = (pairs - high.astype(jnp.float32)).astype(jnp.bfloat16)
            at = pl.ds(pl.multiple_of(j * RCV_DEV, RCV_DEV), RCV_DEV)
            high_ref[i * SHOT_DEV : (i + 1) * SHOT_DEV, at] = high
            low_ref[i * SHOT_DEV : (i + 1) * SHOT_DEV, at] = low
            return carry

        lax.fori_loop(0, rcv_blocks, tile, 0)
    ones_rcv = jnp.ones((16, rcv_blocks * RCV_DEV), jnp.bfloat16)
    ones_shot = jnp.ones((16, shot_blocks * SHOT_DEV), jnp.bfloat16)
    shot_count_ref[...] = (across(ones_rcv, high_ref[...]) + across(ones_rcv, low_ref[...]))[:8]
    rcv_count_ref[...] = (along(ones_shot, high_ref[...]) + along(ones_shot, low_ref[...]))[:8]


def pair_counts(index_every, shot_blocks, rcv_blocks):
    shots, rcvs = shot_blocks * SHOT_DEV, rcv_blocks * RCV_DEV
    return pl.pallas_call(
        functools.partial(pairs_kernel, shot_blocks, rcv_blocks),
        out_shape=[
            jax.ShapeDtypeStruct((shots, rcvs), jnp.bfloat16),
            jax.ShapeDtypeStruct((shots, rcvs), jnp.bfloat16),
            jax.ShapeDtypeStruct((8, shots), jnp.float32),
            jax.ShapeDtypeStruct((8, rcvs), jnp.float32),
        ],
        compiler_params=pltpu.CompilerParams(vmem_limit_bytes=VMEM_BYTES),
        cost_estimate=pl.CostEstimate(
            flops=2 * shots * rcvs * index_every.shape[2], bytes_accessed=4 * shots * rcvs, transcendentals=0
        ),
    )(index_every)


def solve_kernel(shot_blocks, rcv_blocks, groups, *refs):
    high_ref, low_ref, shot_count_ref, rcv_count_ref, out = refs[groups:]
    bins = out.shape[1]

    def total(places, lanes):
        sums = [functools.reduce(lambda a, b: a + b, [part[k, :, lanes] for k in places]) for part in refs[:groups]]
        return jnp.concatenate(sums, axis=0)

    of_shot, of_rcv = slice(0, SHOT_DEV), slice(SHOT_DEV, SHOT_DEV + RCV_DEV)
    shot_logs = jnp.concatenate(
        [total([i * rcv_blocks + j for j in range(rcv_blocks)], of_shot) for i in range(shot_blocks)], axis=1
    )
    rcv_logs = jnp.concatenate(
        [total([i * rcv_blocks + j for i in range(shot_blocks)], of_rcv) for j in range(rcv_blocks)], axis=1
    )
    shot_count = shot_count_ref[0:1, :]
    rcv_count = rcv_count_ref[0:1, :]

    def times(terms, product):
        first = terms.astype(jnp.bfloat16).astype(jnp.float32)
        rest = terms - first
        second = rest.astype(jnp.bfloat16).astype(jnp.float32)
        stack = jnp.concatenate([first, second, rest - second], axis=0).astype(jnp.bfloat16)
        out = product(stack, high_ref[...]) + product(stack, low_ref[...])
        return out[:bins] + out[bins : 2 * bins] + out[2 * bins :]

    shot_terms = shot_logs / shot_count
    rcv_terms = (rcv_logs - times(shot_terms, along)) / rcv_count
    for _ in range(SWEEPS - 1):
        shot_terms = (shot_logs - times(rcv_terms, across)) / shot_count
        rcv_terms = (rcv_logs - times(shot_terms, along)) / rcv_count
    for i in range(shot_blocks):
        for j in range(rcv_blocks):
            out[i * rcv_blocks + j, :, :SHOT_DEV] = shot_terms[:, i * SHOT_DEV : (i + 1) * SHOT_DEV]
            out[i * rcv_blocks + j, :, SHOT_DEV:] = rcv_terms[:, j * RCV_DEV : (j + 1) * RCV_DEV]


def solve(parts, counts, shot_blocks, rcv_blocks):
    devices, bins, lanes = parts[0].shape
    whole = (devices, bins * len(parts), lanes)
    return pl.pallas_call(
        functools.partial(solve_kernel, shot_blocks, rcv_blocks, len(parts)),
        out_shape=jax.ShapeDtypeStruct(whole, jnp.float32),
        compiler_params=pltpu.CompilerParams(vmem_limit_bytes=VMEM_BYTES),
    )(*parts, *counts)


def turn_kernel(groups, back, shot_out, rcv_out):
    devices, owned, lanes = back.shape
    part = owned // groups
    for g in range(groups):
        block = back[:, g * part : (g + 1) * part, :].reshape(devices * part, lanes)
        at = slice(g * devices * part, (g + 1) * devices * part)
        shot_out[:, at] = block[:, :SHOT_DEV].T
        rcv_out[:, at] = block[:, SHOT_DEV:].T


def turn(back, groups):
    bins = back.shape[0] * back.shape[1]
    return pl.pallas_call(
        functools.partial(turn_kernel, groups),
        out_shape=[
            jax.ShapeDtypeStruct((SHOT_DEV, bins), jnp.float32),
            jax.ShapeDtypeStruct((RCV_DEV, bins), jnp.float32),
        ],
        compiler_params=pltpu.CompilerParams(vmem_limit_bytes=VMEM_BYTES),
    )(back)


def shards(traces, trace_shot, trace_rcv, fold_count):
    slot_total = traces.shape[2]
    samples_count = traces.shape[3]
    bins_count = samples_count // 2
    shot_blocks = lax.axis_size("shot")
    rcv_blocks = lax.axis_size("rcv")
    device_total = shot_blocks * rcv_blocks
    groups = GROUPS
    while bins_count % (groups * device_total * 8):
        groups //= 2
    group_bins = bins_count // groups
    exchange = functools.partial(
        lax.all_to_all, axis_name=("shot", "rcv"), split_axis=0, concat_axis=0, tiled=True
    )
    table = dft_tables(samples_count, bins_count)
    alive = jnp.arange(slot_total, dtype=jnp.int32) < fold_count[0, 0]
    index = jnp.where(alive, jnp.stack([trace_shot[0, 0], trace_rcv[0, 0]]), -1)
    index_every = exchange(jnp.broadcast_to(index[None], (device_total,) + index.shape))
    parts = []
    for g in range(groups):
        sums = spectra_sums(traces[0, 0], jnp.asarray(table[:, g * group_bins : (g + 1) * group_bins]), index)
        parts.append(exchange(sums.reshape(device_total, group_bins // device_total, SHOT_DEV + RCV_DEV)))
    counts = pair_counts(index_every, shot_blocks, rcv_blocks)
    back = exchange(solve(parts, counts, shot_blocks, rcv_blocks))
    return tuple(turn(back, groups))


def solution(mesh):
    return jax.shard_map(
        shards,
        mesh=mesh,
        in_specs=(
            P("shot", "rcv", None, None),
            P("shot", "rcv", None),
            P("shot", "rcv", None),
            P("shot", "rcv"),
        ),
        out_specs=(P("shot", None), P("rcv", None)),
        check_vma=False,
    )
```

time: 145 us -> 101 us (0.70)
  Pallas kernels: 63.6 us -> 40.8 us
  waiting for transfers between devices: 21 us -> 8.22 us
  blocking collectives: 40.3 us -> 29.7 us
  starting transfers between devices: 12.5 us -> 16.1 us
  local copies, waits for them, and re-layouts: 5.12 us -> 3.04 us
    pallas_call x2 -> x4, Pallas kernels: 53.5 us -> 30.7 us  [the longest x2 26.8 us: spectra_sums(): pl.pallas_call(functools.partial(spectra_kernel, 1.0 / samples), in_specs...]
    all_to_all x3, waiting for transfers between devices: 21 us -> 8.22 us  [the longest x2 8.08 us: shards(): exchange(sums.reshape(device_total, group_bins // device_total, SHOT_DEV...]
    all_to_all x2 -> x1, blocking collectives: 40.3 us -> 29.7 us  [shards(): back = exchange(solve(parts, counts, shot_blocks, rcv_blocks))]
    all_to_all x3, starting transfers between devices: 12.5 us -> 16.1 us  [the longest x2 8.79 us: shards(): exchange(sums.reshape(device_total, group_bins // device_total, SHOT_DEV...]
  transfers between devices with their start and end apart: 3 -> 3, of which waited for: 2 -> 3; matrix products, arithmetic and copies ran while one was open for 1% -> 0% of each run, Pallas kernels for 42% -> 37%
where the time goes in v2:
time: 101 us; the launch traced here: 99.9 us
  Pallas kernels  40.8 us (40%)
  blocking collectives  29.7 us (29%)
  starting transfers between devices  16.1 us (16%)
  waiting for transfers between devices  8.22 us (8%)
  local copies, waits for them, and re-layouts  3.04 us (3%)
  between operations  1.35 us (1%)
    all_to_all x1, blocking collectives, shards(): back = exchange(solve(parts, counts, shot_blocks, rcv_blocks))  29.7 us
    pallas_call x2, Pallas kernels, spectra_sums(): pl.pallas_call(functools.partial(spectra_kernel, 1.0 / samples), in_specs...  26.8 us
    pallas_call x1, Pallas kernels, pair_counts(): pl.pallas_call(functools.partial(pairs_kernel, shot_blocks, rcv_blocks),...  10.1 us
    all_to_all x2, starting transfers between devices, shards(): exchange(sums.reshape(device_total, group_bins // device_total, SHOT_DEV...  8.79 us
    all_to_all x2, waiting for transfers between devices, shards(): exchange(sums.reshape(device_total, group_bins // device_total, SHOT_DEV...  8.08 us
    all_to_all x1, starting transfers between devices, shards(): exchange(jnp.broadcast_to(index[None], (device_total,) + index.shape))  7.3 us
    pallas_call x1, Pallas kernels, solve(): pl.pallas_call(functools.partial(solve_kernel, shot_blocks, rcv_blocks, l...  2.69 us
    unnamed x6, local copies, waits for them, and re-layouts  2.2 us
  transfers between devices with their start and end apart: 3, of which 3 were waited for; matrix products, arithmetic and copies ran while one was open for 0% of the time, Pallas kernels for 37%

profile of v2, /device:TPU:0, one launch (start us, length us, event | category | flops | bytes accessed | tf_op | source)
XLA Modules:
  0.0 99.9 jit_solution(13803097792893421587)
XLA Ops:
  1.3 0.7 add_select_fusion.index_ref
  2.0 0.0 copy-start.2
  2.0 0.8 broadcast_in_dim.16
  2.9 7.3 %all-to-all-start.2 = ((s32[32,2,1536]{2,1,0:T(2,128)}), s32[32,2,1536]{2,1,0:T(2,128)S(1)}, u32[]{:S(2)}, u32[]{:S(2)}) async-start(s32[32,2,1536]{2,1,0:T(2,128)} %broadcast_in_dim.16), calls=%async_computation.2 | async-start | bytes 786432 | tf_op jit(solution)/shard_map/all_to_all | solution.py:233
  10.2 0.0 copy-done.2
  10.2 13.4 %shard_map.78 = f32[512,256]{1,0:T(8,128)} custom-call(bf16[1536,2048]{1,0:T(8,128)(2,1)} %bitcast.11, bf16[2,512,2048]{2,1,0:T(8,128)(2,1)} %constant.7.clone.table_hbm, s32[2,1536]{1,0:T(2,128)} %copy-done.2), custom_call_target="tpu_custom_call" | custom-call | flops 6442450944 | bytes 4194304 | tf_op jit(solution)/shard_map/pallas_call | solution.py:83
  23.6 0.1 all-to-all-done.2.index_ref
  23.7 5.9 %all-to-all-start.1 = ((f32[32,16,256]{2,1,0:T(8,128)}), f32[32,16,256]{2,1,0:T(8,128)S(1)}, u32[]{:S(2)}, u32[]{:S(2)}) async-start(f32[32,16,256]{2,1,0:T(8,128)} %bitcast.8), calls=%async_computation.1 | async-start | bytes 1048576 | tf_op jit(solution)/shard_map/all_to_all | solution.py:237
  29.6 13.4 %shard_map.77 = f32[512,256]{1,0:T(8,128)} custom-call(bf16[1536,2048]{1,0:T(8,128)(2,1)} %bitcast.12, bf16[2,512,2048]{2,1,0:T(8,128)(2,1)} %constant.6.clone.table_hbm, s32[2,1536]{1,0:T(2,128)} %copy-done.2), custom_call_target="tpu_custom_call" | custom-call | flops 6442450944 | bytes 4194304 | tf_op jit(solution)/shard_map/pallas_call | solution.py:83
  43.0 2.8 %all-to-all-done.1.refs_1_ = f32[32,16,256]{2,1,0:T(8,128)S(1)} async-done(((f32[32,16,256]{2,1,0:T(8,128)}), f32[32,16,256]{2,1,0:T(8,128)S(1)}, u32[]{:S(2)}, u32[]{:S(2)}) %all-to-all-start.1) | async-done | bytes 524320 | tf_op jit(solution)/shard_map/all_to_all | solution.py:237
  45.8 2.9 %all-to-all-start = ((f32[32,16,256]{2,1,0:T(8,128)}), f32[32,16,256]{2,1,0:T(8,128)S(1)}, u32[]{:S(2)}, u32[]{:S(2)}) async-start(f32[32,16,256]{2,1,0:T(8,128)} %bitcast.7), calls=%async_computation | async-start | bytes 1048576 | tf_op jit(solution)/shard_map/all_to_all | solution.py:237
  48.7 10.1 %shard_map.79 = (bf16[512,1024]{1,0:T(8,128)(2,1)S(1)}, bf16[512,1024]{1,0:T(8,128)(2,1)S(1)}, f32[8,512]{1,0:T(8,128)S(1)}, f32[8,1024]{1,0:T(8,128)S(1)}) custom-call(s32[32,2,1536]{2,1,0:T(2,128)S(1)} %all-to-all-done.2.index_ref), custom_call_target="tpu_custom_call" | custom-call | flops 1610612736 | bytes 2097152 | tf_op jit(solution)/shard_map/pallas_call | solution.py:132
  58.8 0.0 copy-start
  58.8 1.0 copy-done
  59.8 5.3 %all-to-all-done.refs_0_ = f32[32,16,256]{2,1,0:T(8,128)S(1)} async-done(((f32[32,16,256]{2,1,0:T(8,128)}), f32[32,16,256]{2,1,0:T(8,128)S(1)}, u32[]{:S(2)}, u32[]{:S(2)}) %all-to-all-start) | async-done | bytes 524320 | tf_op jit(solution)/shard_map/all_to_all | solution.py:237
  65.1 0.0 copy-start.1
  65.1 1.2 %copy-done.1 = bf16[512,1024]{1,0:T(8,128)(2,1)S(1)} copy-done((bf16[512,1024]{1,0:T(8,128)(2,1)S(1)}, bf16[512,1024]{1,0:T(8,128)(2,1)}, u32[]{:S(2)}) %copy-start.1) | copy-done | bytes 1048600
  66.3 2.7 %shard_map.80 = f32[32,32,256]{2,1,0:T(8,128)S(1)} custom-call(f32[32,16,256]{2,1,0:T(8,128)S(1)} %all-to-all-done.refs_0_, f32[32,16,256]{2,1,0:T(8,128)S(1)} %all-to-all-done.1.refs_1_, bf16[512,1024]{1,0:T(8,128)(2,1)S(1)} %get-tuple-element.6.refs_2_, bf16[512,1024]{1,0:T(8,128)(2,1)S(1)} %copy-done.1, f32[8,512]{1,0:T(8,128)S(1)} %get-tuple-element.8.refs_4_, ...), custom_call_target="tpu_custom_call" | custom-call | tf_op jit(solution)/shard_map/pallas_call | solution.py:187
  69.0 29.7 %all_to_all.20.back = f32[32,32,256]{2,1,0:T(8,128)S(1)} all-to-all(f32[32,32,256]{2,1,0:T(8,128)S(1)} %shard_map.80), channel_id=1, replica_groups=mesh['shot'=4,'rcv'=8] {'shot','rcv'}, dimensions={0} | all-to-all | bytes 2097152 | tf_op jit(solution)/shard_map/all_to_all | solution.py:239
  98.7 1.2 %shard_map.81 = (f32[128,1024]{1,0:T(8,128)}, f32[128,1024]{1,0:T(8,128)}) custom-call(f32[32,32,256]{2,1,0:T(8,128)S(1)} %all_to_all.20.back), custom_call_target="tpu_custom_call" | custom-call | tf_op jit(solution)/shard_map/pallas_call | solution.py:206
  (1 shorter events, 0.0 us)
Async XLA Ops:
  2.0 8.2 %copy-start.2 = (s32[2,1536]{1,0:T(2,128)}, s32[2,1536]{1,0:T(2,128)S(1)}, u32[]{:S(2)}) copy-start(s32[2,1536]{1,0:T(2,128)S(1)} %add_select_fusion.index_ref) | copy-start | bytes 36868
  2.9 20.8 %all-to-all-start.2 = ((s32[32,2,1536]{2,1,0:T(2,128)}), s32[32,2,1536]{2,1,0:T(2,128)S(1)}, u32[]{:S(2)}, u32[]{:S(2)}) async-start(s32[32,2,1536]{2,1,0:T(2,128)} %broadcast_in_dim.16), calls=%async_computation.2 | async-start | bytes 786432 | tf_op jit(solution)/shard_map/all_to_all | solution.py:233
  23.7 22.1 %all-to-all-start.1 = ((f32[32,16,256]{2,1,0:T(8,128)}), f32[32,16,256]{2,1,0:T(8,128)S(1)}, u32[]{:S(2)}, u32[]{:S(2)}) async-start(f32[32,16,256]{2,1,0:T(8,128)} %bitcast.8), calls=%async_computation.1 | async-start | bytes 1048576 | tf_op jit(solution)/shard_map/all_to_all | solution.py:237
  45.8 19.3 %all-to-all-start = ((f32[32,16,256]{2,1,0:T(8,128)}), f32[32,16,256]{2,1,0:T(8,128)S(1)}, u32[]{:S(2)}, u32[]{:S(2)}) async-start(f32[32,16,256]{2,1,0:T(8,128)} %bitcast.7), calls=%async_computation | async-start | bytes 1048576 | tf_op jit(solution)/shard_map/all_to_all | solution.py:237
  58.8 1.0 copy-start
  65.1 1.2 %copy-start.1 = (bf16[512,1024]{1,0:T(8,128)(2,1)S(1)}, bf16[512,1024]{1,0:T(8,128)(2,1)}, u32[]{:S(2)}) copy-start(bf16[512,1024]{1,0:T(8,128)(2,1)} %copy-done) | copy-start | bytes 3145732

commit v3 on v2

v3 whole, which is shorter than its diff:
```python
import functools

import jax
import jax.numpy as jnp
import numpy as np
from jax import lax
from jax.experimental import pallas as pl
from jax.experimental.pallas import tpu as pltpu
from jax.sharding import PartitionSpec as P

SHOT_DEV = 128
RCV_DEV = 128
SWEEPS = 3
OWN_ROWS = 8
LANES = 256
ROW_BLOCK = 256
SLOT_BLOCK = 512
VMEM_BYTES = 40 * 1024 * 1024
WHOLE_VMEM_BYTES = 62 * 1024 * 1024


def dft_tables(samples_count, bins_count):
    product = (np.arange(bins_count)[:, None] * np.arange(samples_count)[None, :]) % samples_count
    angle = (np.float32(2.0 * np.pi / samples_count) * product.astype(np.float32)).astype(np.float64)
    both = np.stack([np.cos(angle), np.sin(angle)]).astype(np.float32)
    both = both.reshape(2, bins_count // ROW_BLOCK, ROW_BLOCK, samples_count).transpose(1, 0, 2, 3)
    return both.reshape(-1, 2 * ROW_BLOCK, samples_count).astype(jnp.bfloat16)


def across(a, b):
    return lax.dot_general(a, b, (((1,), (1,)), ((), ())), preferred_element_type=jnp.float32)


def along(a, b):
    return lax.dot_general(a, b, (((1,), (0,)), ((), ())), preferred_element_type=jnp.float32)


def index_lines(slots):
    lines = slots // (2 * LANES)
    return lines, -(-2 * lines // OWN_ROWS) * OWN_ROWS


def spectra_kernel(
    shot_blocks, inv_samples, traces_hbm, table_hbm, shot_ref, rcv_ref, count_ref, sums_ref, traces_ref, table_ref, trace_sem, table_sem
):
    slots = traces_ref.shape[0]
    blocks = table_ref.shape[0]
    pieces = slots // SLOT_BLOCK

    def trace_copy(k):
        span = pl.ds(k * SLOT_BLOCK, SLOT_BLOCK)
        return pltpu.make_async_copy(traces_hbm.at[span], traces_ref.at[span], trace_sem.at[k])

    def table_copy(k):
        return pltpu.make_async_copy(table_hbm.at[k], table_ref.at[k], table_sem.at[k])

    copies = [table_copy(0)] + [trace_copy(k) for k in range(pieces)] + [table_copy(k) for k in range(1, blocks)]
    arrived = []

    def bring(count):
        while len(arrived) < count:
            k = len(arrived)
            if k + 2 < len(copies):
                copies[k + 2].start()
            copies[k].wait()
            arrived.append(k)

    copies[0].start()
    copies[1].start()
    rows = lax.broadcasted_iota(jnp.int32, (SHOT_DEV, slots), 0)
    alive = lax.broadcasted_iota(jnp.int32, (1, slots), 1) < count_ref[0, 0]
    indices = [jnp.where(alive, ref[...], -1) for ref in (shot_ref, rcv_ref)]
    onehot = jnp.concatenate([(index == rows).astype(jnp.float32) for index in indices], axis=0).astype(jnp.bfloat16)
    if shot_blocks:
        lines, taken = index_lines(slots)
        for i in range(shot_blocks):
            ends = [(i % 2 * lines + k) * LANES for k in range(lines)]
            text = [index[:, at : at + LANES].astype(jnp.float32) for index in indices for at in ends]
            text.append(jnp.zeros((taken - 2 * lines, LANES), jnp.float32))
            wide = sums_ref.shape[0] // shot_blocks
            sums_ref[i * wide : (i + 1) * wide, OWN_ROWS:, :] = jnp.broadcast_to(
                jnp.concatenate(text, axis=0)[None], (wide, taken, LANES)
            )

    def add_up(unit, both):
        row, start, stop = unit
        real, imag = both[:ROW_BLOCK], both[ROW_BLOCK:]
        logs = jnp.log((real * real + imag * imag) * inv_samples + 1e-06)
        high = logs.astype(jnp.bfloat16)
        low = (logs - high.astype(jnp.float32)).astype(jnp.bfloat16)
        sums = across(high, onehot[:, start:stop]) + across(low, onehot[:, start:stop])
        if shot_blocks:
            owners = ROW_BLOCK // OWN_ROWS
            at = (slice(row * owners, (row + 1) * owners), slice(0, OWN_ROWS), slice(None))
            sums = sums.reshape(owners, OWN_ROWS, LANES)
        else:
            at = (slice(row * ROW_BLOCK, (row + 1) * ROW_BLOCK), slice(None))
        if start == 0:
            sums_ref[at] = sums
        else:
            sums_ref[at] += sums

    units = [(0, k * SLOT_BLOCK, (k + 1) * SLOT_BLOCK) for k in range(pieces)]
    units += [(row, 0, slots) for row in range(1, blocks)]
    before = None
    for k, unit in enumerate(units):
        bring(2 + k)
        row, start, stop = unit
        both = across(table_ref[row], traces_ref[start:stop, :])
        if before is not None:
            add_up(*before)
        before = (unit, both)
    add_up(*before)


def spectra_sums(traces, table, trace_shot, trace_rcv, fold_count, shot_blocks=0):
    slots, samples = traces.shape
    blocks = table.shape[0]
    bins = blocks * ROW_BLOCK
    shape = (bins // OWN_ROWS, OWN_ROWS + index_lines(slots)[1], LANES) if shot_blocks else (bins, LANES)
    in_vmem = pl.BlockSpec(memory_space=pltpu.VMEM)
    in_hbm = pl.BlockSpec(memory_space=pltpu.HBM)
    return pl.pallas_call(
        functools.partial(spectra_kernel, shot_blocks, 1.0 / samples),
        in_specs=[in_hbm, in_hbm, in_vmem, in_vmem, pl.BlockSpec(memory_space=pltpu.SMEM)],
        out_specs=in_vmem,
        out_shape=jax.ShapeDtypeStruct(shape, jnp.float32),
        scratch_shapes=[
            pltpu.VMEM(traces.shape, traces.dtype),
            pltpu.VMEM(table.shape, table.dtype),
            pltpu.SemaphoreType.DMA((slots // SLOT_BLOCK,)),
            pltpu.SemaphoreType.DMA((blocks,)),
        ],
        compiler_params=pltpu.CompilerParams(vmem_limit_bytes=WHOLE_VMEM_BYTES),
        cost_estimate=pl.CostEstimate(
            flops=4 * slots * samples * bins, bytes_accessed=4 * samples * bins, transcendentals=slots * bins
        ),
    )(traces, table, trace_shot, trace_rcv, fold_count)


def pairs_kernel(lines, mine_ref, other_ref, high_ref, low_ref, shot_count_ref, rcv_count_ref):
    rcv_blocks = high_ref.shape[1] // RCV_DEV
    slots = 2 * lines * LANES
    rows = lax.broadcasted_iota(jnp.int32, (SHOT_DEV, slots), 0).astype(jnp.float32).astype(jnp.bfloat16)
    one = jnp.ones((SHOT_DEV, slots), jnp.bfloat16)
    zero = jnp.zeros_like(one)
    for tile in range(mine_ref.shape[0]):
        halves = [ref[tile] for ref in (mine_ref, other_ref)]
        onehots = []
        for first in (0, lines):
            flat = [half[first + k : first + k + 1, :] for half in halves for k in range(lines)]
            onehots.append(jnp.where(jnp.concatenate(flat, axis=1).astype(jnp.bfloat16) == rows, one, zero))
        pairs = across(*onehots)
        high = pairs.astype(jnp.bfloat16)
        i, j = divmod(tile, rcv_blocks)
        place = (slice(i * SHOT_DEV, (i + 1) * SHOT_DEV), slice(j * RCV_DEV, (j + 1) * RCV_DEV))
        high_ref[place] = high
        low_ref[place] = (pairs - high.astype(jnp.float32)).astype(jnp.bfloat16)
    ones_rcv = jnp.ones((16, high_ref.shape[1]), jnp.bfloat16)
    ones_shot = jnp.ones((16, high_ref.shape[0]), jnp.bfloat16)
    shot_count_ref[...] = (across(ones_rcv, high_ref[...]) + across(ones_rcv, low_ref[...]))[:8]
    rcv_count_ref[...] = (along(ones_shot, high_ref[...]) + along(ones_shot, low_ref[...]))[:8]


def pair_counts(mine, other, lines, shot_blocks, rcv_blocks):
    shots, rcvs = shot_blocks * SHOT_DEV, rcv_blocks * RCV_DEV
    return pl.pallas_call(
        functools.partial(pairs_kernel, lines),
        out_shape=[
            jax.ShapeDtypeStruct((shots, rcvs), jnp.bfloat16),
            jax.ShapeDtypeStruct((shots, rcvs), jnp.bfloat16),
            jax.ShapeDtypeStruct((8, shots), jnp.float32),
            jax.ShapeDtypeStruct((8, rcvs), jnp.float32),
        ],
        compiler_params=pltpu.CompilerParams(vmem_limit_bytes=VMEM_BYTES),
        cost_estimate=pl.CostEstimate(
            flops=4 * shots * rcvs * lines * LANES, bytes_accessed=4 * shots * rcvs, transcendentals=0
        ),
    )(mine, other)


def solve_kernel(shot_blocks, rcv_blocks, own_rows, *refs):
    groups = len(own_rows)
    high_ref, low_ref, shot_count_ref, rcv_count_ref, out = refs[groups:]
    bins = out.shape[1] * 2 // 3

    def total(places, lanes):
        sums = [
            functools.reduce(lambda a, b: a + b, [part[k, :count, lanes] for k in places])
            for part, count in zip(refs, own_rows)
        ]
        return jnp.concatenate(sums, axis=0)

    of_shot, of_rcv = slice(0, SHOT_DEV), slice(SHOT_DEV, SHOT_DEV + RCV_DEV)
    shot_logs = jnp.concatenate(
        [total([i * rcv_blocks + j for j in range(rcv_blocks)], of_shot) for i in range(shot_blocks)], axis=1
    )
    rcv_logs = jnp.concatenate(
        [total([i * rcv_blocks + j for i in range(shot_blocks)], of_rcv) for j in range(rcv_blocks)], axis=1
    )
    shot_count = shot_count_ref[0:1, :]
    rcv_count = rcv_count_ref[0:1, :]

    def times(terms, product):
        first = terms.astype(jnp.bfloat16).astype(jnp.float32)
        rest = terms - first
        second = rest.astype(jnp.bfloat16).astype(jnp.float32)
        stack = jnp.concatenate([first, second, rest - second], axis=0).astype(jnp.bfloat16)
        out = product(stack, high_ref[...]) + product(stack, low_ref[...])
        return out[:bins] + out[bins : 2 * bins] + out[2 * bins :]

    shot_terms = shot_logs / shot_count
    rcv_terms = (rcv_logs - times(shot_terms, along)) / rcv_count
    for _ in range(SWEEPS - 1):
        shot_terms = (shot_logs - times(rcv_terms, across)) / shot_count
        rcv_terms = (rcv_logs - times(shot_terms, along)) / rcv_count
    half = bins // 2
    for i in range(shot_blocks):
        mine = rcv_terms[(i % 2) * half : (i % 2 + 1) * half]
        for j in range(rcv_blocks):
            out[i * rcv_blocks + j, :bins, :] = shot_terms[:, i * SHOT_DEV : (i + 1) * SHOT_DEV]
            out[i * rcv_blocks + j, bins:, :] = mine[:, j * RCV_DEV : (j + 1) * RCV_DEV]


def solve(parts, counts, own_rows, shot_blocks, rcv_blocks):
    return pl.pallas_call(
        functools.partial(solve_kernel, shot_blocks, rcv_blocks, own_rows),
        out_shape=jax.ShapeDtypeStruct((parts[0].shape[0], sum(own_rows) * 3 // 2, SHOT_DEV), jnp.float32),
        compiler_params=pltpu.CompilerParams(vmem_limit_bytes=VMEM_BYTES),
    )(*parts, *counts)


def turn_kernel(own_rows, even_ref, back, other, shot_out, rcv_out):
    devices, owned = back.shape[0], back.shape[1] * 2 // 3
    mine = back[:, owned:, :]
    even = even_ref[0] == 1
    rcv_back = jnp.concatenate([jnp.where(even, mine, other[...]), jnp.where(even, other[...], mine)], axis=1)
    row, at = 0, 0
    for count in own_rows:
        rows, row = slice(row, row + count), row + count
        columns, at = slice(at, at + devices * count), at + devices * count
        shot_out[:, columns] = back[:, rows, :].reshape(devices * count, SHOT_DEV).T
        rcv_out[:, columns] = rcv_back[:, rows, :].reshape(devices * count, RCV_DEV).T


def turn(even, back, other, own_rows):
    bins = back.shape[0] * back.shape[1] * 2 // 3
    return pl.pallas_call(
        functools.partial(turn_kernel, own_rows),
        in_specs=[pl.BlockSpec(memory_space=pltpu.SMEM)] + [pl.BlockSpec(memory_space=pltpu.VMEM)] * 2,
        out_shape=[
            jax.ShapeDtypeStruct((SHOT_DEV, bins), jnp.float32),
            jax.ShapeDtypeStruct((RCV_DEV, bins), jnp.float32),
        ],
        compiler_params=pltpu.CompilerParams(vmem_limit_bytes=VMEM_BYTES),
    )(even, back, other)


def shards(traces, trace_shot, trace_rcv, fold_count):
    slot_total = traces.shape[2]
    samples_count = traces.shape[3]
    bins_count = samples_count // 2
    shot_blocks = lax.axis_size("shot")
    rcv_blocks = lax.axis_size("rcv")
    device_total = shot_blocks * rcv_blocks
    owned = bins_count // device_total
    own_rows = [OWN_ROWS] + ([owned - OWN_ROWS] if owned > OWN_ROWS else [])
    exchange = functools.partial(
        lax.all_to_all, axis_name=("shot", "rcv"), split_axis=0, concat_axis=0, tiled=True
    )
    swap = [(i, i ^ 1) for i in range(shot_blocks)]
    table = dft_tables(samples_count, bins_count)
    lines, taken = index_lines(slot_total)
    parts, at = [], 0
    for rows in own_rows:
        blocks = rows * device_total // ROW_BLOCK
        sums = spectra_sums(
            traces[0, 0],
            jnp.asarray(table[at : at + blocks]),
            trace_shot[0],
            trace_rcv[0],
            fold_count,
            0 if at else shot_blocks,
        )
        parts.append(exchange(sums if at == 0 else sums.reshape(device_total, rows, LANES)))
        at += blocks
    mine = parts[0][:, OWN_ROWS:, :]
    counts = pair_counts(mine, lax.ppermute(mine, "shot", swap), lines, shot_blocks, rcv_blocks)
    back = exchange(solve(parts, counts, own_rows, shot_blocks, rcv_blocks))
    other = lax.ppermute(back[:, owned:, :], "shot", swap)
    even = (1 - lax.axis_index("shot") % 2).astype(jnp.int32).reshape(1)
    return tuple(turn(even, back, other, own_rows))


def solution(mesh):
    return jax.shard_map(
        shards,
        mesh=mesh,
        in_specs=(
            P("shot", "rcv", None, None),
            P("shot", "rcv", None),
            P("shot", "rcv", None),
            P("shot", "rcv"),
        ),
        out_specs=(P("shot", None), P("rcv", None)),
        check_vma=False,
    )
```

time: 101 us -> 93.5 us (0.926)
  waiting for transfers between devices: 8.22 us -> 17.9 us
  Pallas kernels: 40.8 us -> 33.9 us
  blocking collectives: 29.7 us -> 24 us
  starting transfers between devices: 16.1 us -> 13.5 us
    pallas_call x5, Pallas kernels: 40.8 us -> 33.9 us  [the longest x2 25.8 us: spectra_sums(): pl.pallas_call(functools.partial(spectra_kernel, shot_blocks, 1.0 / sampl...]
    all_to_all x3 -> x2, waiting for transfers between devices: 8.22 us -> 14.9 us  [shards(): exchange(sums if at == 0 else sums.reshape(device_total, rows, LANES))]
    all_to_all x1, blocking collectives: 29.7 us -> 24 us  [shards(): back = exchange(solve(parts, counts, own_rows, shot_blocks, rcv_blocks))]
    ppermute x0 -> x2, waiting for transfers between devices: none -> 3.01 us  [the longest x1 1.51 us: shards(): other = lax.ppermute(back[:, owned:, :], 'shot', swap)]
    all_to_all x3 -> x2, starting transfers between devices: 16.1 us -> 13.4 us  [shards(): exchange(sums if at == 0 else sums.reshape(device_total, rows, LANES))]
    unnamed x6 -> x4, local copies, waits for them, and re-layouts: 2.2 us -> 2.21 us
  transfers between devices with their start and end apart: 3 -> 4, of which waited for: 3 -> 3; matrix products, arithmetic and copies ran while one was open for 0% -> 0% of each run, Pallas kernels for 37% -> 23%
where the time goes in v3:
time: 93.5 us; the launch traced here: 93 us
  Pallas kernels  33.9 us (36%)
  blocking collectives  24 us (26%)
  waiting for transfers between devices  17.9 us (19%)
  starting transfers between devices  13.5 us (14%)
  local copies, waits for them, and re-layouts  2.24 us (2%)
  between operations  1.36 us (1%)
    pallas_call x2, Pallas kernels, spectra_sums(): pl.pallas_call(functools.partial(spectra_kernel, shot_blocks, 1.0 / sampl...  25.8 us
    all_to_all x1, blocking collectives, shards(): back = exchange(solve(parts, counts, own_rows, shot_blocks, rcv_blocks))  24 us
    all_to_all x2, waiting for transfers between devices, shards(): exchange(sums if at == 0 else sums.reshape(device_total, rows, LANES))  14.9 us
    all_to_all x2, starting transfers between devices, shards(): exchange(sums if at == 0 else sums.reshape(device_total, rows, LANES))  13.4 us
    pallas_call x1, Pallas kernels, pair_counts(): pl.pallas_call(functools.partial(pairs_kernel, lines), out_shape=[jax.Sha...  4.21 us
    pallas_call x1, Pallas kernels, solve(): pl.pallas_call(functools.partial(solve_kernel, shot_blocks, rcv_blocks, o...  2.67 us
    unnamed x4, local copies, waits for them, and re-layouts  2.21 us
  transfers between devices with their start and end apart: 4, of which 3 were waited for; matrix products, arithmetic and copies ran while one was open for 0% of the time, Pallas kernels for 23%

profile of v3, /device:TPU:0, one launch (start us, length us, event | category | flops | bytes accessed | tf_op | source)
XLA Modules:
  0.0 93.0 jit_solution(6562946329150234617)
XLA Ops:
  1.3 8.9 %shard_map.77 = f32[32,16,256]{2,1,0:T(8,128)} custom-call(bf16[1536,2048]{1,0:T(8,128)(2,1)} %bitcast.6, bf16[1,512,2048]{2,1,0:T(8,128)(2,1)} %constant.23.clone.table_hbm, s32[1,1536]{1,0:T(1,128)} %bitcast.8, s32[1,1536]{1,0:T(1,128)} %bitcast.10, s32[1,1]{1,0:T(1,128)S(6)} %copy.8.count_ref), custom_call_target="tpu_custom_call" | custom-call | flops 3221225472 | bytes 2097152 | tf_op jit(solution)/shard_map/pallas_call | solution.py:123
  10.2 7.5 %all-to-all-start = ((f32[32,16,256]{2,1,0:T(8,128)}), f32[32,16,256]{2,1,0:T(8,128)S(1)}, u32[]{:S(2)}, u32[]{:S(2)}) async-start(f32[32,16,256]{2,1,0:T(8,128)} %shard_map.77), calls=%async_computation | async-start | bytes 1048576 | tf_op jit(solution)/shard_map/all_to_all | solution.py:285
  17.7 16.9 %shard_map.78 = f32[768,256]{1,0:T(8,128)} custom-call(bf16[1536,2048]{1,0:T(8,128)(2,1)} %bitcast.7, bf16[3,512,2048]{2,1,0:T(8,128)(2,1)} %constant.24.clone.table_hbm, s32[1,1536]{1,0:T(1,128)} %bitcast.9, s32[1,1536]{1,0:T(1,128)} %bitcast.11, s32[1,1]{1,0:T(1,128)S(6)} %copy.8.count_ref), custom_call_target="tpu_custom_call" | custom-call | flops 9663676416 | bytes 6291456 | tf_op jit(solution)/shard_map/pallas_call | solution.py:123
  34.6 0.0 all-to-all-done.refs_0_
  34.6 5.9 %all-to-all-start.1 = ((f32[32,24,256]{2,1,0:T(8,128)}), f32[32,24,256]{2,1,0:T(8,128)S(1)}, u32[]{:S(2)}, u32[]{:S(2)}) async-start(f32[32,24,256]{2,1,0:T(8,128)} %bitcast.5), calls=%async_computation.1 | async-start | bytes 1572864 | tf_op jit(solution)/shard_map/all_to_all | solution.py:285
  40.5 0.1 collective-permute-start
  40.6 1.5 %collective-permute-done.other_ref = f32[32,8,256]{2,1,0:T(8,128)S(1)} collective-permute-done((f32[32,8,256]{2,1,0:T(8,128)S(1)}, f32[32,8,256]{2,1,0:T(8,128)S(1)}, u32[]{:S(2)}, u32[]{:S(2)}) %collective-permute-start) | collective-permute-done | bytes 262176 | tf_op jit(solution)/shard_map/ppermute | solution.py:288
  42.1 4.2 %shard_map.79 = (bf16[512,1024]{1,0:T(8,128)(2,1)S(1)}, bf16[512,1024]{1,0:T(8,128)(2,1)S(1)}, f32[8,512]{1,0:T(8,128)S(1)}, f32[8,1024]{1,0:T(8,128)S(1)}) custom-call(f32[32,8,256]{2,1,0:T(8,128)S(1)} %slice.8.mine_ref, f32[32,8,256]{2,1,0:T(8,128)S(1)} %collective-permute-done.other_ref), custom_call_target="tpu_custom_call" | custom-call | flops 1610612736 | bytes 2097152 | tf_op jit(solution)/shard_map/pallas_call | solution.py:167
  46.3 0.0 copy-start
  46.3 1.0 %copy-done = bf16[512,1024]{1,0:T(8,128)(2,1)} copy-done((bf16[512,1024]{1,0:T(8,128)(2,1)}, bf16[512,1024]{1,0:T(8,128)(2,1)S(1)}, u32[]{:S(2)}) %copy-start) | copy-done | bytes 1048600
  47.3 14.9 %all-to-all-done.1.refs_1_ = f32[32,24,256]{2,1,0:T(8,128)S(1)} async-done(((f32[32,24,256]{2,1,0:T(8,128)}), f32[32,24,256]{2,1,0:T(8,128)S(1)}, u32[]{:S(2)}, u32[]{:S(2)}) %all-to-all-start.1) | async-done | bytes 786464 | tf_op jit(solution)/shard_map/all_to_all | solution.py:285
  62.2 0.0 copy-start.1
  62.2 1.2 %copy-done.1 = bf16[512,1024]{1,0:T(8,128)(2,1)S(1)} copy-done((bf16[512,1024]{1,0:T(8,128)(2,1)S(1)}, bf16[512,1024]{1,0:T(8,128)(2,1)}, u32[]{:S(2)}) %copy-start.1) | copy-done | bytes 1048600
  63.5 2.7 %shard_map.80 = f32[32,48,128]{2,1,0:T(8,128)S(1)} custom-call(f32[32,16,256]{2,1,0:T(8,128)S(1)} %all-to-all-done.refs_0_, f32[32,24,256]{2,1,0:T(8,128)S(1)} %all-to-all-done.1.refs_1_, bf16[512,1024]{1,0:T(8,128)(2,1)S(1)} %get-tuple-element.6.refs_2_, bf16[512,1024]{1,0:T(8,128)(2,1)S(1)} %copy-done.1, f32[8,512]{1,0:T(8,128)S(1)} %get-tuple-element.8.refs_4_, ...), custom_call_target="tpu_custom_call" | custom-call | tf_op jit(solution)/shard_map/pallas_call | solution.py:226
  66.1 24.0 %all_to_all.15.back = f32[32,48,128]{2,1,0:T(8,128)S(1)} all-to-all(f32[32,48,128]{2,1,0:T(8,128)S(1)} %shard_map.80), channel_id=1, replica_groups=mesh['shot'=4,'rcv'=8] {'shot','rcv'}, dimensions={0} | all-to-all | bytes 1572864 | tf_op jit(solution)/shard_map/all_to_all | solution.py:289
  90.2 0.1 collective-permute-start.1
  90.3 1.5 %collective-permute-done.1.other = f32[32,16,128]{2,1,0:T(8,128)S(1)} collective-permute-done((f32[32,16,128]{2,1,0:T(8,128)S(1)}, f32[32,16,128]{2,1,0:T(8,128)S(1)}, u32[]{:S(2)}, u32[]{:S(2)}) %collective-permute-start.1) | collective-permute-done | bytes 262176 | tf_op jit(solution)/shard_map/ppermute | solution.py:290
  91.8 1.2 %shard_map.81 = (f32[128,1024]{1,0:T(8,128)}, f32[128,1024]{1,0:T(8,128)}) custom-call(s32[1]{0:T(128)} %bitcast.even_ref, f32[32,48,128]{2,1,0:T(8,128)S(1)} %all_to_all.15.back, f32[32,16,128]{2,1,0:T(8,128)S(1)} %collective-permute-done.1.other), custom_call_target="tpu_custom_call" | custom-call | tf_op jit(solution)/shard_map/pallas_call | solution.py:248
  (2 shorter events, 0.0 us)
Async XLA Ops:
  10.2 24.4 %all-to-all-start = ((f32[32,16,256]{2,1,0:T(8,128)}), f32[32,16,256]{2,1,0:T(8,128)S(1)}, u32[]{:S(2)}, u32[]{:S(2)}) async-start(f32[32,16,256]{2,1,0:T(8,128)} %shard_map.77), calls=%async_computation | async-start | bytes 1048576 | tf_op jit(solution)/shard_map/all_to_all | solution.py:285
  34.6 27.6 %all-to-all-start.1 = ((f32[32,24,256]{2,1,0:T(8,128)}), f32[32,24,256]{2,1,0:T(8,128)S(1)}, u32[]{:S(2)}, u32[]{:S(2)}) async-start(f32[32,24,256]{2,1,0:T(8,128)} %bitcast.5), calls=%async_computation.1 | async-start | bytes 1572864 | tf_op jit(solution)/shard_map/all_to_all | solution.py:285
  40.5 1.6 %collective-permute-start = (f32[32,8,256]{2,1,0:T(8,128)S(1)}, f32[32,8,256]{2,1,0:T(8,128)S(1)}, u32[]{:S(2)}, u32[]{:S(2)}) collective-permute-start(f32[32,8,256]{2,1,0:T(8,128)S(1)} %slice.8.mine_ref), channel_id=1, source_target_pairs={{0,8},{8,0},{16,24},{24,16},{1,9},{9,1},{17,25},{25,17},{2,10},{10... | collective-permute-start | bytes 786440 | tf_op jit(solution)/shard_map/ppermute | solution.py:288
  46.3 1.0 %copy-start = (bf16[512,1024]{1,0:T(8,128)(2,1)}, bf16[512,1024]{1,0:T(8,128)(2,1)S(1)}, u32[]{:S(2)}) copy-start(bf16[512,1024]{1,0:T(8,128)(2,1)S(1)} %get-tuple-element.7.refs_3_) | copy-start | bytes 3145732
  62.2 1.2 %copy-start.1 = (bf16[512,1024]{1,0:T(8,128)(2,1)S(1)}, bf16[512,1024]{1,0:T(8,128)(2,1)}, u32[]{:S(2)}) copy-start(bf16[512,1024]{1,0:T(8,128)(2,1)} %copy-done) | copy-start | bytes 3145732
  90.2 1.6 %collective-permute-start.1 = (f32[32,16,128]{2,1,0:T(8,128)S(1)}, f32[32,16,128]{2,1,0:T(8,128)S(1)}, u32[]{:S(2)}, u32[]{:S(2)}) collective-permute-start(f32[32,16,128]{2,1,0:T(8,128)S(1)} %slice.9), channel_id=1, source_target_pairs={{0,8},{8,0},{16,24},{24,16},{1,9},{9,1},{17,25},{25,17},{2,10},{10... | collective-permute-start | bytes 786440 | tf_op jit(solution)/shard_map/ppermute | solution.py:290

commit v4 on v3

--- a/solution.py
+++ b/solution.py
@@ -19,12 +19,19 @@
 WHOLE_VMEM_BYTES = 62 * 1024 * 1024
 
 
+FOLDS = 4
+QUARTERS = (0, 2, 1, 3)
+
+
 def dft_tables(samples_count, bins_count):
-    product = (np.arange(bins_count)[:, None] * np.arange(samples_count)[None, :]) % samples_count
+    bins = np.concatenate([np.arange(over, bins_count, FOLDS) for over in QUARTERS])
+    product = (bins[:, None] * np.arange(samples_count)[None, :]) % samples_count
     angle = (np.float32(2.0 * np.pi / samples_count) * product.astype(np.float32)).astype(np.float64)
     both = np.stack([np.cos(angle), np.sin(angle)]).astype(np.float32)
     both = both.reshape(2, bins_count // ROW_BLOCK, ROW_BLOCK, samples_count).transpose(1, 0, 2, 3)
-    return both.reshape(-1, 2 * ROW_BLOCK, samples_count).astype(jnp.bfloat16)
+    both = both.reshape(-1, 2 * ROW_BLOCK, samples_count).astype(jnp.bfloat16)
+    even = bins_count // ROW_BLOCK // 2
+    return both[:even, :, : samples_count // FOLDS], both[even:]
 
 
 def across(a, b):
@@ -40,25 +47,30 @@
     return lines, -(-2 * lines // OWN_ROWS) * OWN_ROWS
 
 
-def spectra_kernel(
-    shot_blocks, inv_samples, traces_hbm, table_hbm, shot_ref, rcv_ref, count_ref, sums_ref, traces_ref, table_ref, trace_sem, table_sem
-):
-    slots = traces_ref.shape[0]
-    blocks = table_ref.shape[0]
+def spectra_kernel(shot_blocks, inv_samples, folds, counts, traces_hbm, *refs):
+    tables = len(counts)
+    table_hbms, refs = refs[:tables], refs[tables:]
+    shot_ref, rcv_ref, count_ref, sums_ref, traces_ref, folded_ref, trace_sem = refs[:7]
+    table_refs, table_sems = refs[7 : 7 + tables], refs[7 + tables :]
+    slots, samples = traces_ref.shape
     pieces = slots // SLOT_BLOCK
+    spans = [(k * SLOT_BLOCK, (k + 1) * SLOT_BLOCK) for k in range(pieces)]
 
     def trace_copy(k):
         span = pl.ds(k * SLOT_BLOCK, SLOT_BLOCK)
         return pltpu.make_async_copy(traces_hbm.at[span], traces_ref.at[span], trace_sem.at[k])
 
-    def table_copy(k):
-        return pltpu.make_async_copy(table_hbm.at[k], table_ref.at[k], table_sem.at[k])
-
-    copies = [table_copy(0)] + [trace_copy(k) for k in range(pieces)] + [table_copy(k) for k in range(1, blocks)]
+    def table_copy(table, k):
+        return pltpu.make_async_copy(table_hbms[table].at[k], table_refs[table].at[k], table_sems[table].at[k])
+
+    blocks = [(table, k) for table in range(tables) for k in range(counts[table])]
+    early = min(2, len(blocks))
+    order = [blocks[0], 0] + blocks[1:early] + list(range(1, pieces)) + blocks[early:]
+    copies = [table_copy(*what) if isinstance(what, tuple) else trace_copy(what) for what in order]
     arrived = []
 
-    def bring(count):
-        while len(arrived) < count:
+    def bring(*needed):
+        while len(arrived) <= max(order.index(what) for what in needed):
             k = len(arrived)
             if k + 2 < len(copies):
                 copies[k + 2].start()
@@ -100,42 +112,57 @@
         else:
             sums_ref[at] += sums
 
-    units = [(0, k * SLOT_BLOCK, (k + 1) * SLOT_BLOCK) for k in range(pieces)]
-    units += [(row, 0, slots) for row in range(1, blocks)]
+    def fold(start, stop):
+        wide = samples // FOLDS
+        parts = [traces_ref[start:stop, k * wide : (k + 1) * wide].astype(jnp.float32) for k in range(FOLDS)]
+        outer, inner = parts[0] + parts[2], parts[1] + parts[3]
+        for sign in sorted(set(folds)):
+            total = outer + inner if sign > 0 else outer - inner
+            folded_ref[sign, start:stop, :] = total.astype(jnp.bfloat16)
+
+    units = [(place, *span) for span in spans for place in range(early)]
+    units += [(place, 0, slots) for place in range(early, len(blocks))]
     before = None
-    for k, unit in enumerate(units):
-        bring(2 + k)
-        row, start, stop = unit
-        both = across(table_ref[row], traces_ref[start:stop, :])
+    for place, start, stop in units:
+        table, k = blocks[place]
+        bring(blocks[place], min((stop - 1) // SLOT_BLOCK, pieces - 1))
+        if folds and place == 0:
+            fold(start, stop)
+        if folds and table == 0:
+            both = across(table_refs[0][k], folded_ref[folds[k], start:stop, :])
+        else:
+            both = across(table_refs[table][k], traces_ref[start:stop, :])
         if before is not None:
             add_up(*before)
-        before = (unit, both)
+        before = ((place, start, stop), both)
     add_up(*before)
 
 
-def spectra_sums(traces, table, trace_shot, trace_rcv, fold_count, shot_blocks=0):
+def spectra_sums(traces, tables, folds, trace_shot, trace_rcv, fold_count, shot_blocks=0):
     slots, samples = traces.shape
-    blocks = table.shape[0]
-    bins = blocks * ROW_BLOCK
+    counts = tuple(table.shape[0] for table in tables)
+    bins = sum(counts) * ROW_BLOCK
     shape = (bins // OWN_ROWS, OWN_ROWS + index_lines(slots)[1], LANES) if shot_blocks else (bins, LANES)
     in_vmem = pl.BlockSpec(memory_space=pltpu.VMEM)
     in_hbm = pl.BlockSpec(memory_space=pltpu.HBM)
+    macs = sum(table.size for table in tables) * slots
     return pl.pallas_call(
-        functools.partial(spectra_kernel, shot_blocks, 1.0 / samples),
-        in_specs=[in_hbm, in_hbm, in_vmem, in_vmem, pl.BlockSpec(memory_space=pltpu.SMEM)],
+        functools.partial(spectra_kernel, shot_blocks, 1.0 / samples, folds, counts),
+        in_specs=[in_hbm] * (1 + len(tables)) + [in_vmem, in_vmem, pl.BlockSpec(memory_space=pltpu.SMEM)],
         out_specs=in_vmem,
         out_shape=jax.ShapeDtypeStruct(shape, jnp.float32),
         scratch_shapes=[
             pltpu.VMEM(traces.shape, traces.dtype),
-            pltpu.VMEM(table.shape, table.dtype),
+            pltpu.VMEM((2, slots, samples // FOLDS), traces.dtype),
             pltpu.SemaphoreType.DMA((slots // SLOT_BLOCK,)),
-            pltpu.SemaphoreType.DMA((blocks,)),
-        ],
+        ]
+        + [pltpu.VMEM(table.shape, table.dtype) for table in tables]
+        + [pltpu.SemaphoreType.DMA((count,)) for count in counts],
         compiler_params=pltpu.CompilerParams(vmem_limit_bytes=WHOLE_VMEM_BYTES),
         cost_estimate=pl.CostEstimate(
-            flops=4 * slots * samples * bins, bytes_accessed=4 * samples * bins, transcendentals=slots * bins
+            flops=2 * macs, bytes_accessed=2 * (traces.size + macs // slots), transcendentals=slots * bins
         ),
-    )(traces, table, trace_shot, trace_rcv, fold_count)
+    )(traces, *tables, trace_shot, trace_rcv, fold_count)
 
 
 def pairs_kernel(lines, mine_ref, other_ref, high_ref, low_ref, shot_count_ref, rcv_count_ref):
@@ -230,17 +257,19 @@
     )(*parts, *counts)
 
 
-def turn_kernel(own_rows, even_ref, back, other, shot_out, rcv_out):
+def turn_kernel(own_rows, even_ref, back, other, shot_out, rcv_out, shot_rows, rcv_rows):
     devices, owned = back.shape[0], back.shape[1] * 2 // 3
     mine = back[:, owned:, :]
     even = even_ref[0] == 1
     rcv_back = jnp.concatenate([jnp.where(even, mine, other[...]), jnp.where(even, other[...], mine)], axis=1)
-    row, at = 0, 0
-    for count in own_rows:
-        rows, row = slice(row, row + count), row + count
-        columns, at = slice(at, at + devices * count), at + devices * count
-        shot_out[:, columns] = back[:, rows, :].reshape(devices * count, SHOT_DEV).T
-        rcv_out[:, columns] = rcv_back[:, rows, :].reshape(devices * count, RCV_DEV).T
+    quarter = devices * owned // FOLDS
+    for taken, rows_ref, out in ((back[:, :owned, :], shot_rows, shot_out), (rcv_back, rcv_rows, rcv_out)):
+        ends = [sum(own_rows[:k]) for k in range(len(own_rows) + 1)]
+        flat = [taken[:, a:b, :].reshape(devices * (b - a), out.shape[0]) for a, b in zip(ends, ends[1:])]
+        flat = jnp.concatenate(flat, axis=0)
+        for k, over in enumerate(QUARTERS):
+            rows_ref[pl.ds(over, quarter, stride=FOLDS), :] = flat[k * quarter : (k + 1) * quarter]
+        out[...] = rows_ref[...].T
 
 
 def turn(even, back, other, own_rows):
@@ -252,6 +281,7 @@
             jax.ShapeDtypeStruct((SHOT_DEV, bins), jnp.float32),
             jax.ShapeDtypeStruct((RCV_DEV, bins), jnp.float32),
         ],
+        scratch_shapes=[pltpu.VMEM((bins, SHOT_DEV), jnp.float32), pltpu.VMEM((bins, RCV_DEV), jnp.float32)],
         compiler_params=pltpu.CompilerParams(vmem_limit_bytes=VMEM_BYTES),
     )(even, back, other)
 
@@ -269,21 +299,24 @@
         lax.all_to_all, axis_name=("shot", "rcv"), split_axis=0, concat_axis=0, tiled=True
     )
     swap = [(i, i ^ 1) for i in range(shot_blocks)]
-    table = dft_tables(samples_count, bins_count)
+    folded, plain = dft_tables(samples_count, bins_count)
+    signs = [1] * (len(folded) // 2) + [0] * (len(folded) - len(folded) // 2)
     lines, taken = index_lines(slot_total)
     parts, at = [], 0
     for rows in own_rows:
-        blocks = rows * device_total // ROW_BLOCK
+        end = at + rows * device_total // ROW_BLOCK
+        tables = [folded[at:end], plain[max(at - len(folded), 0) : max(end - len(folded), 0)]]
         sums = spectra_sums(
             traces[0, 0],
-            jnp.asarray(table[at : at + blocks]),
+            [jnp.asarray(table) for table in tables if len(table)],
+            tuple(signs[at:end]),
             trace_shot[0],
             trace_rcv[0],
             fold_count,
             0 if at else shot_blocks,
         )
         parts.append(exchange(sums if at == 0 else sums.reshape(device_total, rows, LANES)))
-        at += blocks
+        at = end
     mine = parts[0][:, OWN_ROWS:, :]
     counts = pair_counts(mine, lax.ppermute(mine, "shot", swap), lines, shot_blocks, rcv_blocks)
     back = exchange(solve(parts, counts, own_rows, shot_blocks, rcv_blocks))

time: 93.5 us -> 87.9 us (0.940)
  Pallas kernels: 33.9 us -> 28.3 us
  waiting for transfers between devices: 17.9 us -> 20.2 us
  starting transfers between devices: 13.5 us -> 11.3 us
    pallas_call x2, Pallas kernels: 25.8 us -> 20.2 us  [spectra_sums(): pl.pallas_call(functools.partial(spectra_kernel, shot_blocks, 1.0 / sampl...]
    all_to_all x2, waiting for transfers between devices: 14.9 us -> 17.2 us  [shards(): exchange(sums if at == 0 else sums.reshape(device_total, rows, LANES))]
    all_to_all x2, starting transfers between devices: 13.4 us -> 11.1 us  [shards(): exchange(sums if at == 0 else sums.reshape(device_total, rows, LANES))]
  transfers between devices with their start and end apart: 4 -> 4, of which waited for: 3 -> 4; matrix products, arithmetic and copies ran while one was open for 0% -> 0% of each run, Pallas kernels for 23% -> 21%
where the time goes in v4:
time: 87.9 us; the launch traced here: 87.4 us
  Pallas kernels  28.3 us (32%)
  blocking collectives  24 us (27%)
  waiting for transfers between devices  20.2 us (23%)
  starting transfers between devices  11.3 us (13%)
  local copies, waits for them, and re-layouts  2.24 us (3%)
  between operations  1.35 us (2%)
    all_to_all x1, blocking collectives, shards(): back = exchange(solve(parts, counts, own_rows, shot_blocks, rcv_blocks))  24 us
    pallas_call x2, Pallas kernels, spectra_sums(): pl.pallas_call(functools.partial(spectra_kernel, shot_blocks, 1.0 / sampl...  20.2 us
    all_to_all x2, waiting for transfers between devices, shards(): exchange(sums if at == 0 else sums.reshape(device_total, rows, LANES))  17.2 us
    all_to_all x2, starting transfers between devices, shards(): exchange(sums if at == 0 else sums.reshape(device_total, rows, LANES))  11.1 us
    pallas_call x1, Pallas kernels, pair_counts(): pl.pallas_call(functools.partial(pairs_kernel, lines), out_shape=[jax.Sha...  4.2 us
    pallas_call x1, Pallas kernels, solve(): pl.pallas_call(functools.partial(solve_kernel, shot_blocks, rcv_blocks, o...  2.67 us
    unnamed x4, local copies, waits for them, and re-layouts  2.21 us
  transfers between devices with their start and end apart: 4, of which 4 were waited for; matrix products, arithmetic and copies ran while one was open for 0% of the time, Pallas kernels for 21%

profile of v4, /device:TPU:0, one launch (start us, length us, event | category | flops | bytes accessed | tf_op | source)
XLA Modules:
  0.0 87.4 jit_solution(9692463914290805505)
XLA Ops:
  1.3 6.2 %shard_map.86 = f32[32,16,256]{2,1,0:T(8,128)} custom-call(bf16[1536,2048]{1,0:T(8,128)(2,1)} %bitcast.5, bf16[1,512,512]{2,1,0:T(8,128)(2,1)} %constant.25.clone.refs_0_, s32[1,1536]{1,0:T(1,128)} %bitcast.8, s32[1,1536]{1,0:T(1,128)} %bitcast.10, s32[1,1]{1,0:T(1,128)S(6)} %copy.9.refs_3_.refs_4_), custom_call_target="tpu_custom_call" | custom-call | flops 805306368 | bytes 6815744 | tf_op jit(solution)/shard_map/pallas_call | solution.py:149
  7.5 7.3 %all-to-all-start = ((f32[32,16,256]{2,1,0:T(8,128)}), f32[32,16,256]{2,1,0:T(8,128)S(1)}, u32[]{:S(2)}, u32[]{:S(2)}) async-start(f32[32,16,256]{2,1,0:T(8,128)} %shard_map.86), calls=%async_computation | async-start | bytes 1048576 | tf_op jit(solution)/shard_map/all_to_all | solution.py:318
  14.8 14.1 %shard_map.87 = f32[768,256]{1,0:T(8,128)} custom-call(bf16[1536,2048]{1,0:T(8,128)(2,1)} %bitcast.6, bf16[1,512,512]{2,1,0:T(8,128)(2,1)} %constant.26.clone.refs_0_, bf16[2,512,2048]{2,1,0:T(8,128)(2,1)} %constant.27.clone.refs_1_, s32[1,1536]{1,0:T(1,128)} %bitcast.9, s32[1,1536]{1,0:T(1,128)} %bitcast.11, s32[1,1]{1,0:T(1,128)S(6)} %copy.9.refs_3_.refs_4_), custom_call_target="tpu_custom_call" | custom-call | flops 7247757312 | bytes 11010048 | tf_op jit(solution)/shard_map/pallas_call | solution.py:149
  28.9 2.3 %all-to-all-done.refs_0_ = f32[32,16,256]{2,1,0:T(8,128)S(1)} async-done(((f32[32,16,256]{2,1,0:T(8,128)}), f32[32,16,256]{2,1,0:T(8,128)S(1)}, u32[]{:S(2)}, u32[]{:S(2)}) %all-to-all-start) | async-done | bytes 524320 | tf_op jit(solution)/shard_map/all_to_all | solution.py:318
  31.1 3.8 %all-to-all-start.1 = ((f32[32,24,256]{2,1,0:T(8,128)}), f32[32,24,256]{2,1,0:T(8,128)S(1)}, u32[]{:S(2)}, u32[]{:S(2)}) async-start(f32[32,24,256]{2,1,0:T(8,128)} %bitcast.7), calls=%async_computation.1 | async-start | bytes 1572864 | tf_op jit(solution)/shard_map/all_to_all | solution.py:318
  34.9 0.1 collective-permute-start
  35.1 1.5 %collective-permute-done.other_ref = f32[32,8,256]{2,1,0:T(8,128)S(1)} collective-permute-done((f32[32,8,256]{2,1,0:T(8,128)S(1)}, f32[32,8,256]{2,1,0:T(8,128)S(1)}, u32[]{:S(2)}, u32[]{:S(2)}) %collective-permute-start) | collective-permute-done | bytes 262176 | tf_op jit(solution)/shard_map/ppermute | solution.py:321
  36.5 4.2 %shard_map.88 = (bf16[512,1024]{1,0:T(8,128)(2,1)S(1)}, bf16[512,1024]{1,0:T(8,128)(2,1)S(1)}, f32[8,512]{1,0:T(8,128)S(1)}, f32[8,1024]{1,0:T(8,128)S(1)}) custom-call(f32[32,8,256]{2,1,0:T(8,128)S(1)} %slice.8.mine_ref, f32[32,8,256]{2,1,0:T(8,128)S(1)} %collective-permute-done.other_ref), custom_call_target="tpu_custom_call" | custom-call | flops 1610612736 | bytes 2097152 | tf_op jit(solution)/shard_map/pallas_call | solution.py:194
  40.7 0.0 copy-start
  40.7 1.0 %copy-done = bf16[512,1024]{1,0:T(8,128)(2,1)} copy-done((bf16[512,1024]{1,0:T(8,128)(2,1)}, bf16[512,1024]{1,0:T(8,128)(2,1)S(1)}, u32[]{:S(2)}) %copy-start) | copy-done | bytes 1048600
  41.7 15.0 %all-to-all-done.1.refs_1_ = f32[32,24,256]{2,1,0:T(8,128)S(1)} async-done(((f32[32,24,256]{2,1,0:T(8,128)}), f32[32,24,256]{2,1,0:T(8,128)S(1)}, u32[]{:S(2)}, u32[]{:S(2)}) %all-to-all-start.1) | async-done | bytes 786464 | tf_op jit(solution)/shard_map/all_to_all | solution.py:318
  56.7 0.0 copy-start.1
  56.7 1.2 %copy-done.1 = bf16[512,1024]{1,0:T(8,128)(2,1)S(1)} copy-done((bf16[512,1024]{1,0:T(8,128)(2,1)S(1)}, bf16[512,1024]{1,0:T(8,128)(2,1)}, u32[]{:S(2)}) %copy-start.1) | copy-done | bytes 1048600
  57.9 2.7 %shard_map.89 = f32[32,48,128]{2,1,0:T(8,128)S(1)} custom-call(f32[32,16,256]{2,1,0:T(8,128)S(1)} %all-to-all-done.refs_0_, f32[32,24,256]{2,1,0:T(8,128)S(1)} %all-to-all-done.1.refs_1_, bf16[512,1024]{1,0:T(8,128)(2,1)S(1)} %get-tuple-element.6.refs_2_, bf16[512,1024]{1,0:T(8,128)(2,1)S(1)} %copy-done.1, f32[8,512]{1,0:T(8,128)S(1)} %get-tuple-element.8.refs_4_, ...), custom_call_target="tpu_custom_call" | custom-call | tf_op jit(solution)/shard_map/pallas_call | solution.py:253
  60.6 24.0 %all_to_all.15.back = f32[32,48,128]{2,1,0:T(8,128)S(1)} all-to-all(f32[32,48,128]{2,1,0:T(8,128)S(1)} %shard_map.89), channel_id=1, replica_groups=mesh['shot'=4,'rcv'=8] {'shot','rcv'}, dimensions={0} | all-to-all | bytes 1572864 | tf_op jit(solution)/shard_map/all_to_all | solution.py:322
  84.6 0.1 collective-permute-start.1
  84.7 1.5 %collective-permute-done.1.other = f32[32,16,128]{2,1,0:T(8,128)S(1)} collective-permute-done((f32[32,16,128]{2,1,0:T(8,128)S(1)}, f32[32,16,128]{2,1,0:T(8,128)S(1)}, u32[]{:S(2)}, u32[]{:S(2)}) %collective-permute-start.1) | collective-permute-done | bytes 262176 | tf_op jit(solution)/shard_map/ppermute | solution.py:323
  86.2 1.2 %shard_map.90 = (f32[128,1024]{1,0:T(8,128)}, f32[128,1024]{1,0:T(8,128)}) custom-call(s32[1]{0:T(128)} %bitcast.even_ref, f32[32,48,128]{2,1,0:T(8,128)S(1)} %all_to_all.15.back, f32[32,16,128]{2,1,0:T(8,128)S(1)} %collective-permute-done.1.other), custom_call_target="tpu_custom_call" | custom-call | tf_op jit(solution)/shard_map/pallas_call | solution.py:277
  (2 shorter events, 0.0 us)
Async XLA Ops:
  7.5 23.7 %all-to-all-start = ((f32[32,16,256]{2,1,0:T(8,128)}), f32[32,16,256]{2,1,0:T(8,128)S(1)}, u32[]{:S(2)}, u32[]{:S(2)}) async-start(f32[32,16,256]{2,1,0:T(8,128)} %shard_map.86), calls=%async_computation | async-start | bytes 1048576 | tf_op jit(solution)/shard_map/all_to_all | solution.py:318
  31.1 25.6 %all-to-all-start.1 = ((f32[32,24,256]{2,1,0:T(8,128)}), f32[32,24,256]{2,1,0:T(8,128)S(1)}, u32[]{:S(2)}, u32[]{:S(2)}) async-start(f32[32,24,256]{2,1,0:T(8,128)} %bitcast.7), calls=%async_computation.1 | async-start | bytes 1572864 | tf_op jit(solution)/shard_map/all_to_all | solution.py:318
  34.9 1.6 %collective-permute-start = (f32[32,8,256]{2,1,0:T(8,128)S(1)}, f32[32,8,256]{2,1,0:T(8,128)S(1)}, u32[]{:S(2)}, u32[]{:S(2)}) collective-permute-start(f32[32,8,256]{2,1,0:T(8,128)S(1)} %slice.8.mine_ref), channel_id=1, source_target_pairs={{0,8},{8,0},{16,24},{24,16},{1,9},{9,1},{17,25},{25,17},{2,10},{10... | collective-permute-start | bytes 786440 | tf_op jit(solution)/shard_map/ppermute | solution.py:321
  40.7 1.0 %copy-start = (bf16[512,1024]{1,0:T(8,128)(2,1)}, bf16[512,1024]{1,0:T(8,128)(2,1)S(1)}, u32[]{:S(2)}) copy-start(bf16[512,1024]{1,0:T(8,128)(2,1)S(1)} %get-tuple-element.7.refs_3_) | copy-start | bytes 3145732
  56.7 1.2 %copy-start.1 = (bf16[512,1024]{1,0:T(8,128)(2,1)S(1)}, bf16[512,1024]{1,0:T(8,128)(2,1)}, u32[]{:S(2)}) copy-start(bf16[512,1024]{1,0:T(8,128)(2,1)} %copy-done) | copy-start | bytes 3145732
  84.6 1.6 %collective-permute-start.1 = (f32[32,16,128]{2,1,0:T(8,128)S(1)}, f32[32,16,128]{2,1,0:T(8,128)S(1)}, u32[]{:S(2)}, u32[]{:S(2)}) collective-permute-start(f32[32,16,128]{2,1,0:T(8,128)S(1)} %slice.9), channel_id=1, source_target_pairs={{0,8},{8,0},{16,24},{24,16},{1,9},{9,1},{17,25},{25,17},{2,10},{10... | collective-permute-start | bytes 786440 | tf_op jit(solution)/shard_map/ppermute | solution.py:323

commit v5 on v4

--- a/solution.py
+++ b/solution.py
@@ -11,8 +11,9 @@
 SHOT_DEV = 128
 RCV_DEV = 128
 SWEEPS = 3
-OWN_ROWS = 8
-LANES = 256
+FIRST_ROWS = 16
+TILE_ROWS = 8
+LANES = 128
 ROW_BLOCK = 256
 SLOT_BLOCK = 512
 VMEM_BYTES = 40 * 1024 * 1024
@@ -44,13 +45,17 @@
 
 def index_lines(slots):
     lines = slots // (2 * LANES)
-    return lines, -(-2 * lines // OWN_ROWS) * OWN_ROWS
-
-
-def spectra_kernel(shot_blocks, inv_samples, folds, counts, traces_hbm, *refs):
+    return lines, -(-2 * lines // TILE_ROWS) * TILE_ROWS
+
+
+def spectra_kernel(places, inv_samples, folds, counts, first, last, traces_hbm, *refs):
+    shot_blocks, rcv_blocks = places
     tables = len(counts)
     table_hbms, refs = refs[:tables], refs[tables:]
-    shot_ref, rcv_ref, count_ref, sums_ref, traces_ref, folded_ref, trace_sem = refs[:7]
+    (shot_ref, rcv_ref, count_ref, core_ref), refs = refs[:4], refs[4:]
+    if not first:
+        earlier_ref, refs = refs[0], refs[1:]
+    sums_ref, second_ref, traces_ref, folded_ref, shot_sums, rcv_sums, trace_sem = refs[:7]
     table_refs, table_sems = refs[7 : 7 + tables], refs[7 + tables :]
     slots, samples = traces_ref.shape
     pieces = slots // SLOT_BLOCK
@@ -83,15 +88,16 @@
     alive = lax.broadcasted_iota(jnp.int32, (1, slots), 1) < count_ref[0, 0]
     indices = [jnp.where(alive, ref[...], -1) for ref in (shot_ref, rcv_ref)]
     onehot = jnp.concatenate([(index == rows).astype(jnp.float32) for index in indices], axis=0).astype(jnp.bfloat16)
-    if shot_blocks:
+    owners = shot_blocks * rcv_blocks
+    own = shot_sums.shape[0] // owners
+    if first:
         lines, taken = index_lines(slots)
         for i in range(shot_blocks):
             ends = [(i % 2 * lines + k) * LANES for k in range(lines)]
             text = [index[:, at : at + LANES].astype(jnp.float32) for index in indices for at in ends]
             text.append(jnp.zeros((taken - 2 * lines, LANES), jnp.float32))
-            wide = sums_ref.shape[0] // shot_blocks
-            sums_ref[i * wide : (i + 1) * wide, OWN_ROWS:, :] = jnp.broadcast_to(
-                jnp.concatenate(text, axis=0)[None], (wide, taken, LANES)
+            sums_ref[i * rcv_blocks : (i + 1) * rcv_blocks, own : own + taken, :] = jnp.broadcast_to(
+                jnp.concatenate(text, axis=0)[None], (rcv_blocks, taken, LANES)
             )
 
     def add_up(unit, both):
@@ -101,16 +107,12 @@
         high = logs.astype(jnp.bfloat16)
         low = (logs - high.astype(jnp.float32)).astype(jnp.bfloat16)
         sums = across(high, onehot[:, start:stop]) + across(low, onehot[:, start:stop])
-        if shot_blocks:
-            owners = ROW_BLOCK // OWN_ROWS
-            at = (slice(row * owners, (row + 1) * owners), slice(0, OWN_ROWS), slice(None))
-            sums = sums.reshape(owners, OWN_ROWS, LANES)
-        else:
-            at = (slice(row * ROW_BLOCK, (row + 1) * ROW_BLOCK), slice(None))
-        if start == 0:
-            sums_ref[at] = sums
-        else:
-            sums_ref[at] += sums
+        at = slice(row * ROW_BLOCK, (row + 1) * ROW_BLOCK)
+        for ref, lanes in ((shot_sums, slice(0, SHOT_DEV)), (rcv_sums, slice(SHOT_DEV, SHOT_DEV + RCV_DEV))):
+            if start == 0:
+                ref[at, :] = sums[:, lanes]
+            else:
+                ref[at, :] += sums[:, lanes]
 
     def fold(start, stop):
         wide = samples // FOLDS
@@ -136,24 +138,45 @@
             add_up(*before)
         before = ((place, start, stop), both)
     add_up(*before)
-
-
-def spectra_sums(traces, tables, folds, trace_shot, trace_rcv, fold_count, shot_blocks=0):
+    sums_ref[:, :own, :] = shot_sums[...].reshape(owners, own, SHOT_DEV)
+    of_rcv = rcv_sums[...].reshape(owners, own, RCV_DEV)
+    if last:
+        whole = of_rcv if first else jnp.concatenate([earlier_ref[...], of_rcv], axis=1)
+        half = whole.shape[1] // 2
+        even = core_ref[0] == 0
+        low, high = whole[:, :half, :], whole[:, half:, :]
+        sums_ref[:, sums_ref.shape[1] - half :, :] = jnp.where(even, low, high)
+        second_ref[...] = jnp.where(even, high, low)
+    else:
+        second_ref[...] = of_rcv
+
+
+def spectra_sums(traces, tables, folds, trace_shot, trace_rcv, fold_count, core, places, earlier, last):
+    first = earlier is None
     slots, samples = traces.shape
+    owners = places[0] * places[1]
     counts = tuple(table.shape[0] for table in tables)
     bins = sum(counts) * ROW_BLOCK
-    shape = (bins // OWN_ROWS, OWN_ROWS + index_lines(slots)[1], LANES) if shot_blocks else (bins, LANES)
+    own = bins // owners
+    half = (own + (0 if first else earlier.shape[1])) // 2
+    rows = own + (index_lines(slots)[1] if first else 0) + (half if last else 0)
     in_vmem = pl.BlockSpec(memory_space=pltpu.VMEM)
     in_hbm = pl.BlockSpec(memory_space=pltpu.HBM)
+    in_smem = pl.BlockSpec(memory_space=pltpu.SMEM)
     macs = sum(table.size for table in tables) * slots
     return pl.pallas_call(
-        functools.partial(spectra_kernel, shot_blocks, 1.0 / samples, folds, counts),
-        in_specs=[in_hbm] * (1 + len(tables)) + [in_vmem, in_vmem, pl.BlockSpec(memory_space=pltpu.SMEM)],
-        out_specs=in_vmem,
-        out_shape=jax.ShapeDtypeStruct(shape, jnp.float32),
+        functools.partial(spectra_kernel, places, 1.0 / samples, folds, counts, first, last),
+        in_specs=[in_hbm] * (1 + len(tables)) + [in_vmem, in_vmem, in_smem, in_smem] + [in_vmem] * (not first),
+        out_specs=[in_vmem, in_vmem],
+        out_shape=[
+            jax.ShapeDtypeStruct((owners, rows, SHOT_DEV), jnp.float32),
+            jax.ShapeDtypeStruct((owners, half if last else own, RCV_DEV), jnp.float32),
+        ],
         scratch_shapes=[
             pltpu.VMEM(traces.shape, traces.dtype),
             pltpu.VMEM((2, slots, samples // FOLDS), traces.dtype),
+            pltpu.VMEM((bins, SHOT_DEV), jnp.float32),
+            pltpu.VMEM((bins, RCV_DEV), jnp.float32),
             pltpu.SemaphoreType.DMA((slots // SLOT_BLOCK,)),
         ]
         + [pltpu.VMEM(table.shape, table.dtype) for table in tables]
@@ -162,7 +185,7 @@
         cost_estimate=pl.CostEstimate(
             flops=2 * macs, bytes_accessed=2 * (traces.size + macs // slots), transcendentals=slots * bins
         ),
-    )(traces, *tables, trace_shot, trace_rcv, fold_count)
+    )(traces, *tables, trace_shot, trace_rcv, fold_count, core, *([] if first else [earlier]))
 
 
 def pairs_kernel(lines, mine_ref, other_ref, high_ref, low_ref, shot_count_ref, rcv_count_ref):
@@ -211,20 +234,24 @@
     high_ref, low_ref, shot_count_ref, rcv_count_ref, out = refs[groups:]
     bins = out.shape[1] * 2 // 3
 
-    def total(places, lanes):
-        sums = [
-            functools.reduce(lambda a, b: a + b, [part[k, :count, lanes] for k in places])
-            for part, count in zip(refs, own_rows)
-        ]
-        return jnp.concatenate(sums, axis=0)
-
-    of_shot, of_rcv = slice(0, SHOT_DEV), slice(SHOT_DEV, SHOT_DEV + RCV_DEV)
-    shot_logs = jnp.concatenate(
-        [total([i * rcv_blocks + j for j in range(rcv_blocks)], of_shot) for i in range(shot_blocks)], axis=1
-    )
-    rcv_logs = jnp.concatenate(
-        [total([i * rcv_blocks + j for i in range(shot_blocks)], of_rcv) for j in range(rcv_blocks)], axis=1
-    )
+    def total(terms):
+        return functools.reduce(lambda a, b: a + b, terms)
+
+    def shot_sum(i):
+        tiles = range(i * rcv_blocks, (i + 1) * rcv_blocks)
+        return jnp.concatenate(
+            [total([part[k, :count, :] for k in tiles]) for part, count in zip(refs, own_rows)], axis=0
+        )
+
+    def rcv_sum(j):
+        at = slice(refs[groups - 1].shape[1] - bins // 2, refs[groups - 1].shape[1])
+        halves = [range(parity, shot_blocks, 2) for parity in range(2)]
+        return jnp.concatenate(
+            [total([refs[groups - 1][i * rcv_blocks + j, at, :] for i in half]) for half in halves], axis=0
+        )
+
+    shot_logs = jnp.concatenate([shot_sum(i) for i in range(shot_blocks)], axis=1)
+    rcv_logs = jnp.concatenate([rcv_sum(j) for j in range(rcv_blocks)], axis=1)
     shot_count = shot_count_ref[0:1, :]
     rcv_count = rcv_count_ref[0:1, :]
 
@@ -257,10 +284,10 @@
     )(*parts, *counts)
 
 
-def turn_kernel(own_rows, even_ref, back, other, shot_out, rcv_out, shot_rows, rcv_rows):
+def turn_kernel(own_rows, core_ref, back, other, shot_out, rcv_out, shot_rows, rcv_rows):
     devices, owned = back.shape[0], back.shape[1] * 2 // 3
     mine = back[:, owned:, :]
-    even = even_ref[0] == 1
+    even = core_ref[0] == 0
     rcv_back = jnp.concatenate([jnp.where(even, mine, other[...]), jnp.where(even, other[...], mine)], axis=1)
     quarter = devices * owned // FOLDS
     for taken, rows_ref, out in ((back[:, :owned, :], shot_rows, shot_out), (rcv_back, rcv_rows, rcv_out)):
@@ -272,7 +299,7 @@
         out[...] = rows_ref[...].T
 
 
-def turn(even, back, other, own_rows):
+def turn(core, back, other, own_rows):
     bins = back.shape[0] * back.shape[1] * 2 // 3
     return pl.pallas_call(
         functools.partial(turn_kernel, own_rows),
@@ -283,7 +310,7 @@
         ],
         scratch_shapes=[pltpu.VMEM((bins, SHOT_DEV), jnp.float32), pltpu.VMEM((bins, RCV_DEV), jnp.float32)],
         compiler_params=pltpu.CompilerParams(vmem_limit_bytes=VMEM_BYTES),
-    )(even, back, other)
+    )(core, back, other)
 
 
 def shards(traces, trace_shot, trace_rcv, fold_count):
@@ -294,7 +321,7 @@
     rcv_blocks = lax.axis_size("rcv")
     device_total = shot_blocks * rcv_blocks
     owned = bins_count // device_total
-    own_rows = [OWN_ROWS] + ([owned - OWN_ROWS] if owned > OWN_ROWS else [])
+    own_rows = [FIRST_ROWS, owned - FIRST_ROWS] if owned > FIRST_ROWS else [owned]
     exchange = functools.partial(
         lax.all_to_all, axis_name=("shot", "rcv"), split_axis=0, concat_axis=0, tiled=True
     )
@@ -302,27 +329,34 @@
     folded, plain = dft_tables(samples_count, bins_count)
     signs = [1] * (len(folded) // 2) + [0] * (len(folded) - len(folded) // 2)
     lines, taken = index_lines(slot_total)
-    parts, at = [], 0
-    for rows in own_rows:
+    here = lax.axis_index("shot")
+    core = (here % 2).astype(jnp.int32).reshape(1)
+    parts, at, second = [], 0, None
+    for k, rows in enumerate(own_rows):
         end = at + rows * device_total // ROW_BLOCK
         tables = [folded[at:end], plain[max(at - len(folded), 0) : max(end - len(folded), 0)]]
-        sums = spectra_sums(
+        last = k == len(own_rows) - 1
+        sums, second = spectra_sums(
             traces[0, 0],
             [jnp.asarray(table) for table in tables if len(table)],
             tuple(signs[at:end]),
             trace_shot[0],
             trace_rcv[0],
             fold_count,
-            0 if at else shot_blocks,
+            core,
+            (shot_blocks, rcv_blocks),
+            second,
+            last,
         )
-        parts.append(exchange(sums if at == 0 else sums.reshape(device_total, rows, LANES)))
+        if last:
+            sums = sums.at[:, sums.shape[1] - owned // 2 :, :].add(lax.ppermute(second, "shot", swap))
+        parts.append(exchange(sums))
         at = end
-    mine = parts[0][:, OWN_ROWS:, :]
+    mine = parts[0][:, own_rows[0] : own_rows[0] + taken, :]
     counts = pair_counts(mine, lax.ppermute(mine, "shot", swap), lines, shot_blocks, rcv_blocks)
     back = exchange(solve(parts, counts, own_rows, shot_blocks, rcv_blocks))
     other = lax.ppermute(back[:, owned:, :], "shot", swap)
-    even = (1 - lax.axis_index("shot") % 2).astype(jnp.int32).reshape(1)
-    return tuple(turn(even, back, other, own_rows))
+    return tuple(turn(core, back, other, own_rows))
 
 
 def solution(mesh):

time: 87.9 us -> 85.7 us (0.975)
  waiting for transfers between devices: 20.2 us -> 13.9 us
  starting transfers between devices: 11.3 us -> 13.7 us
  other arithmetic: 0 us -> 1.69 us
    all_to_all x2, waiting for transfers between devices: 17.2 us -> 9.46 us  [shards(): parts.append(exchange(sums))]
    all_to_all x2, starting transfers between devices: 11.1 us -> 13.2 us  [shards(): parts.append(exchange(sums))]
    scatter-add x0 -> x1, other arithmetic: none -> 1.69 us  [shards(): sums.at[:, sums.shape[1] - owned // 2:, :]]
    ppermute x0 -> x1, waiting for transfers between devices: none -> 1.5 us  [shards(): lax.ppermute(second, 'shot', swap)]
  transfers between devices with their start and end apart: 4 -> 5, of which waited for: 4 -> 5; matrix products, arithmetic and copies ran while one was open for 0% -> 2% of each run, Pallas kernels for 21% -> 20%
where the time goes in v5:
time: 85.7 us; the launch traced here: 85.2 us
  Pallas kernels  28.2 us (33%)
  blocking collectives  24 us (28%)
  waiting for transfers between devices  13.9 us (16%)
  starting transfers between devices  13.7 us (16%)
  local copies, waits for them, and re-layouts  2.25 us (3%)
  other arithmetic  1.69 us (2%)
  between operations  1.35 us (2%)
    all_to_all x1, blocking collectives, shards(): back = exchange(solve(parts, counts, own_rows, shot_blocks, rcv_blocks))  24 us
    pallas_call x2, Pallas kernels, spectra_sums(): pl.pallas_call(functools.partial(spectra_kernel, places, 1.0 / samples, f...  20.2 us
    all_to_all x2, starting transfers between devices, shards(): parts.append(exchange(sums))  13.2 us
    all_to_all x2, waiting for transfers between devices, shards(): parts.append(exchange(sums))  9.46 us
    pallas_call x1, Pallas kernels, pair_counts(): pl.pallas_call(functools.partial(pairs_kernel, lines), out_shape=[jax.Sha...  4.2 us
    pallas_call x1, Pallas kernels, solve(): pl.pallas_call(functools.partial(solve_kernel, shot_blocks, rcv_blocks, o...  2.65 us
    unnamed x4, local copies, waits for them, and re-layouts  2.21 us
  transfers between devices with their start and end apart: 5, of which 5 were waited for; matrix products, arithmetic and copies ran while one was open for 2% of the time, Pallas kernels for 20%

profile of v5, /device:TPU:0, one launch (start us, length us, event | category | flops | bytes accessed | tf_op | source)
XLA Modules:
  0.0 85.2 jit_solution(16815126930003887719)
XLA Ops:
  1.3 7.4 %shard_map.77 = (f32[32,32,128]{2,1,0:T(8,128)}, f32[32,16,128]{2,1,0:T(8,128)}) custom-call(bf16[1536,2048]{1,0:T(8,128)(2,1)} %bitcast.4, bf16[2,512,512]{2,1,0:T(8,128)(2,1)} %constant.50.clone.refs_0_, s32[1,1536]{1,0:T(1,128)} %bitcast.6, s32[1,1536]{1,0:T(1,128)} %bitcast.8, s32[1,1]{1,0:T(1,128)S(6)} %copy.9.refs_3_, s32[1]{0:T(128)} %bitcast.refs_4_.core_ref), custom_call_target="tpu_custom_call" | custom-call | flops 1610612736 | bytes 7340032 | tf_op jit(solution)/shard_map/pallas_call | solution.py:167
  8.7 7.3 %all-to-all-start = ((f32[32,32,128]{2,1,0:T(8,128)}), f32[32,32,128]{2,1,0:T(8,128)S(1)}, u32[]{:S(2)}, u32[]{:S(2)}) async-start(f32[32,32,128]{2,1,0:T(8,128)} %get-tuple-element.22), calls=%async_computation | async-start | bytes 1048576 | tf_op jit(solution)/shard_map/all_to_all | solution.py:353
  16.0 12.7 %shard_map.78 = (f32[32,32,128]{2,1,0:T(8,128)}, f32[32,16,128]{2,1,0:T(8,128)}) custom-call(bf16[1536,2048]{1,0:T(8,128)(2,1)} %bitcast.5, bf16[2,512,2048]{2,1,0:T(8,128)(2,1)} %constant.51.clone.refs_0_, s32[1,1536]{1,0:T(1,128)} %bitcast.7, s32[1,1536]{1,0:T(1,128)} %bitcast.9, s32[1,1]{1,0:T(1,128)S(6)} %copy.9.refs_3_, s32[1]{0:T(128)} %bitcast.refs_4_.core_ref, ...), custom_call_target="tpu_custom_call" | custom-call | flops 6442450944 | bytes 10485760 | tf_op jit(solution)/shard_map/pallas_call | solution.py:167
  28.8 0.3 collective-permute-start
  29.1 1.5 %collective-permute-done = f32[32,16,128]{2,1,0:T(8,128)S(1)} collective-permute-done((f32[32,16,128]{2,1,0:T(8,128)}, f32[32,16,128]{2,1,0:T(8,128)S(1)}, u32[]{:S(2)}, u32[]{:S(2)}) %collective-permute-start) | collective-permute-done | bytes 262176 | tf_op jit(solution)/shard_map/ppermute | solution.py:352
  30.6 1.7 %add_dynamic-update-slice_fusion = f32[32,32,128]{2,1,0:T(8,128)} fusion(f32[32,32,128]{2,1,0:T(8,128)} %get-tuple-element.24, f32[32,16,128]{2,1,0:T(8,128)S(1)} %collective-permute-done), kind=kLoop, calls=%fused_computation | loop fusion | flops 65536 | bytes 786432 | tf_op jit(solution)/shard_map/scatter-add | solution.py:352
  32.3 0.1 all-to-all-done.refs_0_
  32.4 5.9 %all-to-all-start.1 = ((f32[32,32,128]{2,1,0:T(8,128)}), f32[32,32,128]{2,1,0:T(8,128)S(1)}, u32[]{:S(2)}, u32[]{:S(2)}) async-start(f32[32,32,128]{2,1,0:T(8,128)} %add_dynamic-update-slice_fusion), calls=%async_computation.1 | async-start | bytes 1048576 | tf_op jit(solution)/shard_map/all_to_all | solution.py:353
  38.3 0.1 collective-permute-start.1
  38.5 1.5 %collective-permute-done.1.other_ref = f32[32,16,128]{2,1,0:T(8,128)S(1)} collective-permute-done((f32[32,16,128]{2,1,0:T(8,128)S(1)}, f32[32,16,128]{2,1,0:T(8,128)S(1)}, u32[]{:S(2)}, u32[]{:S(2)}) %collective-permute-start.1) | collective-permute-done | bytes 262176 | tf_op jit(solution)/shard_map/ppermute | solution.py:356
  39.9 4.2 %shard_map.79 = (bf16[512,1024]{1,0:T(8,128)(2,1)S(1)}, bf16[512,1024]{1,0:T(8,128)(2,1)S(1)}, f32[8,512]{1,0:T(8,128)S(1)}, f32[8,1024]{1,0:T(8,128)S(1)}) custom-call(f32[32,16,128]{2,1,0:T(8,128)S(1)} %slice.33.mine_ref, f32[32,16,128]{2,1,0:T(8,128)S(1)} %collective-permute-done.1.other_ref), custom_call_target="tpu_custom_call" | custom-call | flops 1610612736 | bytes 2097152 | tf_op jit(solution)/shard_map/pallas_call | solution.py:217
  44.1 0.0 copy-start
  44.1 1.0 %copy-done = bf16[512,1024]{1,0:T(8,128)(2,1)} copy-done((bf16[512,1024]{1,0:T(8,128)(2,1)}, bf16[512,1024]{1,0:T(8,128)(2,1)S(1)}, u32[]{:S(2)}) %copy-start) | copy-done | bytes 1048600
  45.1 9.4 %all-to-all-done.1.refs_1_ = f32[32,32,128]{2,1,0:T(8,128)S(1)} async-done(((f32[32,32,128]{2,1,0:T(8,128)}), f32[32,32,128]{2,1,0:T(8,128)S(1)}, u32[]{:S(2)}, u32[]{:S(2)}) %all-to-all-start.1) | async-done | bytes 524320 | tf_op jit(solution)/shard_map/all_to_all | solution.py:353
  54.5 0.0 copy-start.1
  54.5 1.2 %copy-done.1 = bf16[512,1024]{1,0:T(8,128)(2,1)S(1)} copy-done((bf16[512,1024]{1,0:T(8,128)(2,1)S(1)}, bf16[512,1024]{1,0:T(8,128)(2,1)}, u32[]{:S(2)}) %copy-start.1) | copy-done | bytes 1048600
  55.7 2.7 %shard_map.80 = f32[32,48,128]{2,1,0:T(8,128)S(1)} custom-call(f32[32,32,128]{2,1,0:T(8,128)S(1)} %all-to-all-done.refs_0_, f32[32,32,128]{2,1,0:T(8,128)S(1)} %all-to-all-done.1.refs_1_, bf16[512,1024]{1,0:T(8,128)(2,1)S(1)} %get-tuple-element.26.refs_2_, bf16[512,1024]{1,0:T(8,128)(2,1)S(1)} %copy-done.1, f32[8,512]{1,0:T(8,128)S(1)} %get-tuple-element.28.refs_4_, ...), custom_call_target="tpu_custom_call" | custom-call | tf_op jit(solution)/shard_map/pallas_call | solution.py:280
  58.4 24.0 %all_to_all.15.back = f32[32,48,128]{2,1,0:T(8,128)S(1)} all-to-all(f32[32,48,128]{2,1,0:T(8,128)S(1)} %shard_map.80), channel_id=1, replica_groups=mesh['shot'=4,'rcv'=8] {'shot','rcv'}, dimensions={0} | all-to-all | bytes 1572864 | tf_op jit(solution)/shard_map/all_to_all | solution.py:357
  82.4 0.1 collective-permute-start.2
  82.5 1.5 %collective-permute-done.2.other = f32[32,16,128]{2,1,0:T(8,128)S(1)} collective-permute-done((f32[32,16,128]{2,1,0:T(8,128)S(1)}, f32[32,16,128]{2,1,0:T(8,128)S(1)}, u32[]{:S(2)}, u32[]{:S(2)}) %collective-permute-start.2) | collective-permute-done | bytes 262176 | tf_op jit(solution)/shard_map/ppermute | solution.py:358
  84.0 1.2 %shard_map.81 = (f32[128,1024]{1,0:T(8,128)}, f32[128,1024]{1,0:T(8,128)}) custom-call(s32[1]{0:T(128)} %bitcast.refs_4_.core_ref, f32[32,48,128]{2,1,0:T(8,128)S(1)} %all_to_all.15.back, f32[32,16,128]{2,1,0:T(8,128)S(1)} %collective-permute-done.2.other), custom_call_target="tpu_custom_call" | custom-call | tf_op jit(solution)/shard_map/pallas_call | solution.py:304
  (2 shorter events, 0.0 us)
Async XLA Ops:
  8.7 23.7 %all-to-all-start = ((f32[32,32,128]{2,1,0:T(8,128)}), f32[32,32,128]{2,1,0:T(8,128)S(1)}, u32[]{:S(2)}, u32[]{:S(2)}) async-start(f32[32,32,128]{2,1,0:T(8,128)} %get-tuple-element.22), calls=%async_computation | async-start | bytes 1048576 | tf_op jit(solution)/shard_map/all_to_all | solution.py:353
  28.8 1.8 %collective-permute-start = (f32[32,16,128]{2,1,0:T(8,128)}, f32[32,16,128]{2,1,0:T(8,128)S(1)}, u32[]{:S(2)}, u32[]{:S(2)}) collective-permute-start(f32[32,16,128]{2,1,0:T(8,128)} %get-tuple-element.25), channel_id=1, source_target_pairs={{0,8},{8,0},{16,24},{24,16},{1,9},{9,1},{17,25},{25,17},{2,10},{10... | collective-permute-start | bytes 786440 | tf_op jit(solution)/shard_map/ppermute | solution.py:352
  32.4 22.1 %all-to-all-start.1 = ((f32[32,32,128]{2,1,0:T(8,128)}), f32[32,32,128]{2,1,0:T(8,128)S(1)}, u32[]{:S(2)}, u32[]{:S(2)}) async-start(f32[32,32,128]{2,1,0:T(8,128)} %add_dynamic-update-slice_fusion), calls=%async_computation.1 | async-start | bytes 1048576 | tf_op jit(solution)/shard_map/all_to_all | solution.py:353
  38.3 1.6 %collective-permute-start.1 = (f32[32,16,128]{2,1,0:T(8,128)S(1)}, f32[32,16,128]{2,1,0:T(8,128)S(1)}, u32[]{:S(2)}, u32[]{:S(2)}) collective-permute-start(f32[32,16,128]{2,1,0:T(8,128)S(1)} %slice.33.mine_ref), channel_id=1, source_target_pairs={{0,8},{8,0},{16,24},{24,16},{1,9},{9,1},{17,25},{25,17},{2,10},{10... | collective-permute-start | bytes 786440 | tf_op jit(solution)/shard_map/ppermute | solution.py:356
  44.1 1.0 %copy-start = (bf16[512,1024]{1,0:T(8,128)(2,1)}, bf16[512,1024]{1,0:T(8,128)(2,1)S(1)}, u32[]{:S(2)}) copy-start(bf16[512,1024]{1,0:T(8,128)(2,1)S(1)} %get-tuple-element.27.refs_3_) | copy-start | bytes 3145732
  54.5 1.2 %copy-start.1 = (bf16[512,1024]{1,0:T(8,128)(2,1)S(1)}, bf16[512,1024]{1,0:T(8,128)(2,1)}, u32[]{:S(2)}) copy-start(bf16[512,1024]{1,0:T(8,128)(2,1)} %copy-done) | copy-start | bytes 3145732
  82.4 1.6 %collective-permute-start.2 = (f32[32,16,128]{2,1,0:T(8,128)S(1)}, f32[32,16,128]{2,1,0:T(8,128)S(1)}, u32[]{:S(2)}, u32[]{:S(2)}) collective-permute-start(f32[32,16,128]{2,1,0:T(8,128)S(1)} %slice.34), channel_id=1, source_target_pairs={{0,8},{8,0},{16,24},{24,16},{1,9},{9,1},{17,25},{25,17},{2,10},{10... | collective-permute-start | bytes 786440 | tf_op jit(solution)/shard_map/ppermute | solution.py:358

commit v6 on v5

--- a/solution.py
+++ b/solution.py
@@ -24,15 +24,21 @@
 QUARTERS = (0, 2, 1, 3)
 
 
+FOLDS = 4
+QUARTERS = (0, 2, 1, 3)
+SPANS = (4, 4, 2, 1)
+
+
 def dft_tables(samples_count, bins_count):
-    bins = np.concatenate([np.arange(over, bins_count, FOLDS) for over in QUARTERS])
-    product = (bins[:, None] * np.arange(samples_count)[None, :]) % samples_count
-    angle = (np.float32(2.0 * np.pi / samples_count) * product.astype(np.float32)).astype(np.float64)
-    both = np.stack([np.cos(angle), np.sin(angle)]).astype(np.float32)
-    both = both.reshape(2, bins_count // ROW_BLOCK, ROW_BLOCK, samples_count).transpose(1, 0, 2, 3)
-    both = both.reshape(-1, 2 * ROW_BLOCK, samples_count).astype(jnp.bfloat16)
-    even = bins_count // ROW_BLOCK // 2
-    return both[:even, :, : samples_count // FOLDS], both[even:]
+    tables = []
+    for over, span in zip(QUARTERS, SPANS):
+        bins = np.arange(over, bins_count, FOLDS)
+        product = (bins[:, None] * np.arange(samples_count // span)[None, :]) % samples_count
+        angle = (np.float32(2.0 * np.pi / samples_count) * product.astype(np.float32)).astype(np.float64)
+        both = np.stack([np.cos(angle), np.sin(angle)]).astype(np.float32)
+        both = both.reshape(2, len(bins) // ROW_BLOCK, ROW_BLOCK, -1).transpose(1, 0, 2, 3)
+        tables.append(both.reshape(len(both), 2 * ROW_BLOCK, -1).astype(jnp.bfloat16))
+    return tables
 
 
 def across(a, b):
@@ -48,15 +54,15 @@
     return lines, -(-2 * lines // TILE_ROWS) * TILE_ROWS
 
 
-def spectra_kernel(places, inv_samples, folds, counts, first, last, traces_hbm, *refs):
+def spectra_kernel(places, inv_samples, kinds, counts, first, last, traces_hbm, *refs):
     shot_blocks, rcv_blocks = places
     tables = len(counts)
     table_hbms, refs = refs[:tables], refs[tables:]
     (shot_ref, rcv_ref, count_ref, core_ref), refs = refs[:4], refs[4:]
     if not first:
         earlier_ref, refs = refs[0], refs[1:]
-    sums_ref, second_ref, traces_ref, folded_ref, shot_sums, rcv_sums, trace_sem = refs[:7]
-    table_refs, table_sems = refs[7 : 7 + tables], refs[7 + tables :]
+    sums_ref, second_ref, traces_ref, folded_ref, halved_ref, shot_sums, rcv_sums, trace_sem = refs[:8]
+    table_refs, table_sems = refs[8 : 8 + tables], refs[8 + tables :]
     slots, samples = traces_ref.shape
     pieces = slots // SLOT_BLOCK
     spans = [(k * SLOT_BLOCK, (k + 1) * SLOT_BLOCK) for k in range(pieces)]
@@ -117,10 +123,19 @@
     def fold(start, stop):
         wide = samples // FOLDS
         parts = [traces_ref[start:stop, k * wide : (k + 1) * wide].astype(jnp.float32) for k in range(FOLDS)]
-        outer, inner = parts[0] + parts[2], parts[1] + parts[3]
-        for sign in sorted(set(folds)):
-            total = outer + inner if sign > 0 else outer - inner
-            folded_ref[sign, start:stop, :] = total.astype(jnp.bfloat16)
+        for kind in kinds:
+            if kind < 2:
+                outer, inner = parts[0] + parts[2], parts[1] + parts[3]
+                total = outer + inner if kind == 0 else outer - inner
+                folded_ref[kind, start:stop, :] = total.astype(jnp.bfloat16)
+            elif kind == 2:
+                halved_ref[start:stop, :wide] = (parts[0] - parts[2]).astype(jnp.bfloat16)
+                halved_ref[start:stop, wide:] = (parts[1] - parts[3]).astype(jnp.bfloat16)
+
+    def folded(kind, start, stop):
+        if kind < 2:
+            return folded_ref[kind, start:stop, :]
+        return (halved_ref if kind == 2 else traces_ref)[start:stop, :]
 
     units = [(place, *span) for span in spans for place in range(early)]
     units += [(place, 0, slots) for place in range(early, len(blocks))]
@@ -128,12 +143,9 @@
     for place, start, stop in units:
         table, k = blocks[place]
         bring(blocks[place], min((stop - 1) // SLOT_BLOCK, pieces - 1))
-        if folds and place == 0:
+        if place == 0:
             fold(start, stop)
-        if folds and table == 0:
-            both = across(table_refs[0][k], folded_ref[folds[k], start:stop, :])
-        else:
-            both = across(table_refs[table][k], traces_ref[start:stop, :])
+        both = across(table_refs[table][k], folded(kinds[table], start, stop))
         if before is not None:
             add_up(*before)
         before = ((place, start, stop), both)
@@ -151,7 +163,7 @@
         second_ref[...] = of_rcv
 
 
-def spectra_sums(traces, tables, folds, trace_shot, trace_rcv, fold_count, core, places, earlier, last):
+def spectra_sums(traces, tables, kinds, trace_shot, trace_rcv, fold_count, core, places, earlier, last):
     first = earlier is None
     slots, samples = traces.shape
     owners = places[0] * places[1]
@@ -165,7 +177,7 @@
     in_smem = pl.BlockSpec(memory_space=pltpu.SMEM)
     macs = sum(table.size for table in tables) * slots
     return pl.pallas_call(
-        functools.partial(spectra_kernel, places, 1.0 / samples, folds, counts, first, last),
+        functools.partial(spectra_kernel, places, 1.0 / samples, kinds, counts, first, last),
         in_specs=[in_hbm] * (1 + len(tables)) + [in_vmem, in_vmem, in_smem, in_smem] + [in_vmem] * (not first),
         out_specs=[in_vmem, in_vmem],
         out_shape=[
@@ -175,6 +187,7 @@
         scratch_shapes=[
             pltpu.VMEM(traces.shape, traces.dtype),
             pltpu.VMEM((2, slots, samples // FOLDS), traces.dtype),
+            pltpu.VMEM((slots, samples // 2), traces.dtype),
             pltpu.VMEM((bins, SHOT_DEV), jnp.float32),
             pltpu.VMEM((bins, RCV_DEV), jnp.float32),
             pltpu.SemaphoreType.DMA((slots // SLOT_BLOCK,)),
@@ -326,20 +339,23 @@
         lax.all_to_all, axis_name=("shot", "rcv"), split_axis=0, concat_axis=0, tiled=True
     )
     swap = [(i, i ^ 1) for i in range(shot_blocks)]
-    folded, plain = dft_tables(samples_count, bins_count)
-    signs = [1] * (len(folded) // 2) + [0] * (len(folded) - len(folded) // 2)
+    tables = dft_tables(samples_count, bins_count)
     lines, taken = index_lines(slot_total)
     here = lax.axis_index("shot")
     core = (here % 2).astype(jnp.int32).reshape(1)
     parts, at, second = [], 0, None
     for k, rows in enumerate(own_rows):
         end = at + rows * device_total // ROW_BLOCK
-        tables = [folded[at:end], plain[max(at - len(folded), 0) : max(end - len(folded), 0)]]
+        used = []
+        for kind, table in enumerate(tables):
+            start = kind * len(table)
+            used.append((kind, table[max(at - start, 0) : max(end - start, 0)]))
+        used = [(kind, jnp.asarray(table)) for kind, table in used if len(table)]
         last = k == len(own_rows) - 1
         sums, second = spectra_sums(
             traces[0, 0],
-            [jnp.asarray(table) for table in tables if len(table)],
-            tuple(signs[at:end]),
+            [table for _, table in used],
+            tuple(kind for kind, _ in used),
             trace_shot[0],
             trace_rcv[0],
             fold_count,

time: 85.7 us -> 83.8 us (0.978)
  waiting for transfers between devices: 13.9 us -> 15.8 us
  Pallas kernels: 28.2 us -> 26.3 us
  starting transfers between devices: 13.7 us -> 11.9 us
    pallas_call x2, Pallas kernels: 20.2 us -> 18.3 us  [spectra_sums(): pl.pallas_call(functools.partial(spectra_kernel, places, 1.0 / samples, k...]
    all_to_all x2, starting transfers between devices: 13.2 us -> 11.4 us  [shards(): parts.append(exchange(sums))]
    all_to_all x2, waiting for transfers between devices: 9.46 us -> 11.3 us  [shards(): parts.append(exchange(sums))]
  transfers between devices with their start and end apart: 5 -> 5, of which waited for: 5 -> 5; matrix products, arithmetic and copies ran while one was open for 2% -> 2% of each run, Pallas kernels for 20% -> 18%
where the time goes in v6:
time: 83.8 us; the launch traced here: 83.3 us
  Pallas kernels  26.3 us (31%)
  blocking collectives  24 us (29%)
  waiting for transfers between devices  15.8 us (19%)
  starting transfers between devices  11.9 us (14%)
  local copies, waits for them, and re-layouts  2.25 us (3%)
  other arithmetic  1.69 us (2%)
  between operations  1.35 us (2%)
    all_to_all x1, blocking collectives, shards(): back = exchange(solve(parts, counts, own_rows, shot_blocks, rcv_blocks))  24 us
    pallas_call x2, Pallas kernels, spectra_sums(): pl.pallas_call(functools.partial(spectra_kernel, places, 1.0 / samples, k...  18.3 us
    all_to_all x2, starting transfers between devices, shards(): parts.append(exchange(sums))  11.4 us
    all_to_all x2, waiting for transfers between devices, shards(): parts.append(exchange(sums))  11.3 us
    pallas_call x1, Pallas kernels, pair_counts(): pl.pallas_call(functools.partial(pairs_kernel, lines), out_shape=[jax.Sha...  4.22 us
    pallas_call x1, Pallas kernels, solve(): pl.pallas_call(functools.partial(solve_kernel, shot_blocks, rcv_blocks, o...  2.66 us
    unnamed x4, local copies, waits for them, and re-layouts  2.21 us
    scatter-add x1, other arithmetic, shards(): sums.at[:, sums.shape[1] - owned // 2:, :]  1.69 us
  transfers between devices with their start and end apart: 5, of which 5 were waited for; matrix products, arithmetic and copies ran while one was open for 2% of the time, Pallas kernels for 18%

profile of v6, /device:TPU:0, one launch (start us, length us, event | category | flops | bytes accessed | tf_op | source)
XLA Modules:
  0.0 83.3 jit_solution(11252399702788249381)
XLA Ops:
  1.3 7.4 %shard_map.95 = (f32[32,32,128]{2,1,0:T(8,128)}, f32[32,16,128]{2,1,0:T(8,128)}) custom-call(bf16[1536,2048]{1,0:T(8,128)(2,1)} %bitcast.4, bf16[1,512,512]{2,1,0:T(8,128)(2,1)} %constant.54.clone.refs_0_, bf16[1,512,512]{2,1,0:T(8,128)(2,1)} %constant.55.clone.refs_1_, s32[1,1536]{1,0:T(1,128)} %bitcast.6, s32[1,1536]{1,0:T(1,128)} %bitcast.8, ...), custom_call_target="tpu_custom_call" | custom-call | flops 1610612736 | bytes 7340032 | tf_op jit(solution)/shard_map/pallas_call | solution.py:179
  8.7 7.3 %all-to-all-start = ((f32[32,32,128]{2,1,0:T(8,128)}), f32[32,32,128]{2,1,0:T(8,128)S(1)}, u32[]{:S(2)}, u32[]{:S(2)}) async-start(f32[32,32,128]{2,1,0:T(8,128)} %get-tuple-element.22), calls=%async_computation | async-start | bytes 1048576 | tf_op jit(solution)/shard_map/all_to_all | solution.py:369
  16.0 10.9 %shard_map.96 = (f32[32,32,128]{2,1,0:T(8,128)}, f32[32,16,128]{2,1,0:T(8,128)}) custom-call(bf16[1536,2048]{1,0:T(8,128)(2,1)} %bitcast.5, bf16[1,512,1024]{2,1,0:T(8,128)(2,1)} %constant.56.clone.refs_0_, bf16[1,512,2048]{2,1,0:T(8,128)(2,1)} %constant.57.clone.refs_1_, s32[1,1536]{1,0:T(1,128)} %bitcast.7, s32[1,1536]{1,0:T(1,128)} %bitcast.9, ...), custom_call_target="tpu_custom_call" | custom-call | flops 4831838208 | bytes 9437184 | tf_op jit(solution)/shard_map/pallas_call | solution.py:179
  26.9 0.3 collective-permute-start
  27.2 1.5 %collective-permute-done = f32[32,16,128]{2,1,0:T(8,128)S(1)} collective-permute-done((f32[32,16,128]{2,1,0:T(8,128)}, f32[32,16,128]{2,1,0:T(8,128)S(1)}, u32[]{:S(2)}, u32[]{:S(2)}) %collective-permute-start) | collective-permute-done | bytes 262176 | tf_op jit(solution)/shard_map/ppermute | solution.py:368
  28.7 1.7 %add_dynamic-update-slice_fusion = f32[32,32,128]{2,1,0:T(8,128)} fusion(f32[32,32,128]{2,1,0:T(8,128)} %get-tuple-element.24, f32[32,16,128]{2,1,0:T(8,128)S(1)} %collective-permute-done), kind=kLoop, calls=%fused_computation | loop fusion | flops 65536 | bytes 786432 | tf_op jit(solution)/shard_map/scatter-add | solution.py:368
  30.4 2.0 %all-to-all-done.refs_0_ = f32[32,32,128]{2,1,0:T(8,128)S(1)} async-done(((f32[32,32,128]{2,1,0:T(8,128)}), f32[32,32,128]{2,1,0:T(8,128)S(1)}, u32[]{:S(2)}, u32[]{:S(2)}) %all-to-all-start) | async-done | bytes 524320 | tf_op jit(solution)/shard_map/all_to_all | solution.py:369
  32.4 4.0 %all-to-all-start.1 = ((f32[32,32,128]{2,1,0:T(8,128)}), f32[32,32,128]{2,1,0:T(8,128)S(1)}, u32[]{:S(2)}, u32[]{:S(2)}) async-start(f32[32,32,128]{2,1,0:T(8,128)} %add_dynamic-update-slice_fusion), calls=%async_computation.1 | async-start | bytes 1048576 | tf_op jit(solution)/shard_map/all_to_all | solution.py:369
  36.5 0.1 collective-permute-start.1
  36.6 1.5 %collective-permute-done.1.other_ref = f32[32,16,128]{2,1,0:T(8,128)S(1)} collective-permute-done((f32[32,16,128]{2,1,0:T(8,128)S(1)}, f32[32,16,128]{2,1,0:T(8,128)S(1)}, u32[]{:S(2)}, u32[]{:S(2)}) %collective-permute-start.1) | collective-permute-done | bytes 262176 | tf_op jit(solution)/shard_map/ppermute | solution.py:372
  38.1 4.2 %shard_map.97 = (bf16[512,1024]{1,0:T(8,128)(2,1)S(1)}, bf16[512,1024]{1,0:T(8,128)(2,1)S(1)}, f32[8,512]{1,0:T(8,128)S(1)}, f32[8,1024]{1,0:T(8,128)S(1)}) custom-call(f32[32,16,128]{2,1,0:T(8,128)S(1)} %slice.33.mine_ref, f32[32,16,128]{2,1,0:T(8,128)S(1)} %collective-permute-done.1.other_ref), custom_call_target="tpu_custom_call" | custom-call | flops 1610612736 | bytes 2097152 | tf_op jit(solution)/shard_map/pallas_call | solution.py:230
  42.3 0.0 copy-start
  42.3 1.0 %copy-done = bf16[512,1024]{1,0:T(8,128)(2,1)} copy-done((bf16[512,1024]{1,0:T(8,128)(2,1)}, bf16[512,1024]{1,0:T(8,128)(2,1)S(1)}, u32[]{:S(2)}) %copy-start) | copy-done | bytes 1048600
  43.3 9.3 %all-to-all-done.1.refs_1_ = f32[32,32,128]{2,1,0:T(8,128)S(1)} async-done(((f32[32,32,128]{2,1,0:T(8,128)}), f32[32,32,128]{2,1,0:T(8,128)S(1)}, u32[]{:S(2)}, u32[]{:S(2)}) %all-to-all-start.1) | async-done | bytes 524320 | tf_op jit(solution)/shard_map/all_to_all | solution.py:369
  52.6 0.0 copy-start.1
  52.6 1.2 %copy-done.1 = bf16[512,1024]{1,0:T(8,128)(2,1)S(1)} copy-done((bf16[512,1024]{1,0:T(8,128)(2,1)S(1)}, bf16[512,1024]{1,0:T(8,128)(2,1)}, u32[]{:S(2)}) %copy-start.1) | copy-done | bytes 1048600
  53.8 2.7 %shard_map.98 = f32[32,48,128]{2,1,0:T(8,128)S(1)} custom-call(f32[32,32,128]{2,1,0:T(8,128)S(1)} %all-to-all-done.refs_0_, f32[32,32,128]{2,1,0:T(8,128)S(1)} %all-to-all-done.1.refs_1_, bf16[512,1024]{1,0:T(8,128)(2,1)S(1)} %get-tuple-element.26.refs_2_, bf16[512,1024]{1,0:T(8,128)(2,1)S(1)} %copy-done.1, f32[8,512]{1,0:T(8,128)S(1)} %get-tuple-element.28.refs_4_, ...), custom_call_target="tpu_custom_call" | custom-call | tf_op jit(solution)/shard_map/pallas_call | solution.py:293
  56.5 24.0 %all_to_all.15.back = f32[32,48,128]{2,1,0:T(8,128)S(1)} all-to-all(f32[32,48,128]{2,1,0:T(8,128)S(1)} %shard_map.98), channel_id=1, replica_groups=mesh['shot'=4,'rcv'=8] {'shot','rcv'}, dimensions={0} | all-to-all | bytes 1572864 | tf_op jit(solution)/shard_map/all_to_all | solution.py:373
  80.6 0.1 collective-permute-start.2
  80.6 1.5 %collective-permute-done.2.other = f32[32,16,128]{2,1,0:T(8,128)S(1)} collective-permute-done((f32[32,16,128]{2,1,0:T(8,128)S(1)}, f32[32,16,128]{2,1,0:T(8,128)S(1)}, u32[]{:S(2)}, u32[]{:S(2)}) %collective-permute-start.2) | collective-permute-done | bytes 262176 | tf_op jit(solution)/shard_map/ppermute | solution.py:374
  82.2 1.2 %shard_map.99 = (f32[128,1024]{1,0:T(8,128)}, f32[128,1024]{1,0:T(8,128)}) custom-call(s32[1]{0:T(128)} %bitcast.refs_5_.core_ref, f32[32,48,128]{2,1,0:T(8,128)S(1)} %all_to_all.15.back, f32[32,16,128]{2,1,0:T(8,128)S(1)} %collective-permute-done.2.other), custom_call_target="tpu_custom_call" | custom-call | tf_op jit(solution)/shard_map/pallas_call | solution.py:317
  (2 shorter events, 0.0 us)
Async XLA Ops:
  8.7 23.7 %all-to-all-start = ((f32[32,32,128]{2,1,0:T(8,128)}), f32[32,32,128]{2,1,0:T(8,128)S(1)}, u32[]{:S(2)}, u32[]{:S(2)}) async-start(f32[32,32,128]{2,1,0:T(8,128)} %get-tuple-element.22), calls=%async_computation | async-start | bytes 1048576 | tf_op jit(solution)/shard_map/all_to_all | solution.py:369
  26.9 1.8 %collective-permute-start = (f32[32,16,128]{2,1,0:T(8,128)}, f32[32,16,128]{2,1,0:T(8,128)S(1)}, u32[]{:S(2)}, u32[]{:S(2)}) collective-permute-start(f32[32,16,128]{2,1,0:T(8,128)} %get-tuple-element.25), channel_id=1, source_target_pairs={{0,8},{8,0},{16,24},{24,16},{1,9},{9,1},{17,25},{25,17},{2,10},{10... | collective-permute-start | bytes 786440 | tf_op jit(solution)/shard_map/ppermute | solution.py:368
  32.4 20.2 %all-to-all-start.1 = ((f32[32,32,128]{2,1,0:T(8,128)}), f32[32,32,128]{2,1,0:T(8,128)S(1)}, u32[]{:S(2)}, u32[]{:S(2)}) async-start(f32[32,32,128]{2,1,0:T(8,128)} %add_dynamic-update-slice_fusion), calls=%async_computation.1 | async-start | bytes 1048576 | tf_op jit(solution)/shard_map/all_to_all | solution.py:369
  36.5 1.6 %collective-permute-start.1 = (f32[32,16,128]{2,1,0:T(8,128)S(1)}, f32[32,16,128]{2,1,0:T(8,128)S(1)}, u32[]{:S(2)}, u32[]{:S(2)}) collective-permute-start(f32[32,16,128]{2,1,0:T(8,128)S(1)} %slice.33.mine_ref), channel_id=1, source_target_pairs={{0,8},{8,0},{16,24},{24,16},{1,9},{9,1},{17,25},{25,17},{2,10},{10... | collective-permute-start | bytes 786440 | tf_op jit(solution)/shard_map/ppermute | solution.py:372
  42.3 1.0 %copy-start = (bf16[512,1024]{1,0:T(8,128)(2,1)}, bf16[512,1024]{1,0:T(8,128)(2,1)S(1)}, u32[]{:S(2)}) copy-start(bf16[512,1024]{1,0:T(8,128)(2,1)S(1)} %get-tuple-element.27.refs_3_) | copy-start | bytes 3145732
  52.6 1.2 %copy-start.1 = (bf16[512,1024]{1,0:T(8,128)(2,1)S(1)}, bf16[512,1024]{1,0:T(8,128)(2,1)}, u32[]{:S(2)}) copy-start(bf16[512,1024]{1,0:T(8,128)(2,1)} %copy-done) | copy-start | bytes 3145732
  80.6 1.6 %collective-permute-start.2 = (f32[32,16,128]{2,1,0:T(8,128)S(1)}, f32[32,16,128]{2,1,0:T(8,128)S(1)}, u32[]{:S(2)}, u32[]{:S(2)}) collective-permute-start(f32[32,16,128]{2,1,0:T(8,128)S(1)} %slice.34), channel_id=1, source_target_pairs={{0,8},{8,0},{16,24},{24,16},{1,9},{9,1},{17,25},{25,17},{2,10},{10... | collective-permute-start | bytes 786440 | tf_op jit(solution)/shard_map/ppermute | solution.py:374

commit v7 on v6

--- a/solution.py
+++ b/solution.py
@@ -16,6 +16,7 @@
 LANES = 128
 ROW_BLOCK = 256
 SLOT_BLOCK = 512
+DEPTH = 3
 VMEM_BYTES = 40 * 1024 * 1024
 WHOLE_VMEM_BYTES = 62 * 1024 * 1024
 
@@ -83,13 +84,13 @@
     def bring(*needed):
         while len(arrived) <= max(order.index(what) for what in needed):
             k = len(arrived)
-            if k + 2 < len(copies):
-                copies[k + 2].start()
+            if k + DEPTH < len(copies):
+                copies[k + DEPTH].start()
             copies[k].wait()
             arrived.append(k)
 
-    copies[0].start()
-    copies[1].start()
+    for copy in copies[:DEPTH]:
+        copy.start()
     rows = lax.broadcasted_iota(jnp.int32, (SHOT_DEV, slots), 0)
     alive = lax.broadcasted_iota(jnp.int32, (1, slots), 1) < count_ref[0, 0]
     indices = [jnp.where(alive, ref[...], -1) for ref in (shot_ref, rcv_ref)]
@@ -297,33 +298,52 @@
     )(*parts, *counts)
 
 
-def turn_kernel(own_rows, core_ref, back, other, shot_out, rcv_out, shot_rows, rcv_rows):
-    devices, owned = back.shape[0], back.shape[1] * 2 // 3
+def natural(own_rows, taken, rows_ref, out):
+    devices, owned = taken.shape[0], taken.shape[1]
+    quarter = devices * owned // FOLDS
+    ends = [sum(own_rows[:k]) for k in range(len(own_rows) + 1)]
+    flat = [taken[:, a:b, :].reshape(devices * (b - a), out.shape[0]) for a, b in zip(ends, ends[1:])]
+    flat = jnp.concatenate(flat, axis=0)
+    for k, over in enumerate(QUARTERS):
+        rows_ref[pl.ds(over, quarter, stride=FOLDS), :] = flat[k * quarter : (k + 1) * quarter]
+    out[...] = rows_ref[...].T
+
+
+def turn_shot_kernel(own_rows, back, out, rows_ref):
+    natural(own_rows, back[:, : sum(own_rows), :], rows_ref, out)
+
+
+def turn_rcv_kernel(own_rows, core_ref, mine, other, out, rows_ref):
+    even = core_ref[0] == 0
+    low = jnp.where(even, mine[...], other[...])
+    high = jnp.where(even, other[...], mine[...])
+    natural(own_rows, jnp.concatenate([low, high], axis=1), rows_ref, out)
+
+
+def turn(core, back, swap, own_rows):
+    owned = sum(own_rows)
+    bins = back.shape[0] * owned
+    params = pltpu.CompilerParams(vmem_limit_bytes=VMEM_BYTES)
+    in_vmem = pl.BlockSpec(memory_space=pltpu.VMEM)
+    scratch = [pltpu.VMEM((bins, SHOT_DEV), jnp.float32)]
     mine = back[:, owned:, :]
-    even = core_ref[0] == 0
-    rcv_back = jnp.concatenate([jnp.where(even, mine, other[...]), jnp.where(even, other[...], mine)], axis=1)
-    quarter = devices * owned // FOLDS
-    for taken, rows_ref, out in ((back[:, :owned, :], shot_rows, shot_out), (rcv_back, rcv_rows, rcv_out)):
-        ends = [sum(own_rows[:k]) for k in range(len(own_rows) + 1)]
-        flat = [taken[:, a:b, :].reshape(devices * (b - a), out.shape[0]) for a, b in zip(ends, ends[1:])]
-        flat = jnp.concatenate(flat, axis=0)
-        for k, over in enumerate(QUARTERS):
-            rows_ref[pl.ds(over, quarter, stride=FOLDS), :] = flat[k * quarter : (k + 1) * quarter]
-        out[...] = rows_ref[...].T
-
-
-def turn(core, back, other, own_rows):
-    bins = back.shape[0] * back.shape[1] * 2 // 3
-    return pl.pallas_call(
-        functools.partial(turn_kernel, own_rows),
-        in_specs=[pl.BlockSpec(memory_space=pltpu.SMEM)] + [pl.BlockSpec(memory_space=pltpu.VMEM)] * 2,
-        out_shape=[
-            jax.ShapeDtypeStruct((SHOT_DEV, bins), jnp.float32),
-            jax.ShapeDtypeStruct((RCV_DEV, bins), jnp.float32),
-        ],
-        scratch_shapes=[pltpu.VMEM((bins, SHOT_DEV), jnp.float32), pltpu.VMEM((bins, RCV_DEV), jnp.float32)],
-        compiler_params=pltpu.CompilerParams(vmem_limit_bytes=VMEM_BYTES),
-    )(core, back, other)
+    other = lax.ppermute(mine, "shot", swap)
+    shot_out = pl.pallas_call(
+        functools.partial(turn_shot_kernel, own_rows),
+        in_specs=[in_vmem],
+        out_shape=jax.ShapeDtypeStruct((SHOT_DEV, bins), jnp.float32),
+        scratch_shapes=scratch,
+        compiler_params=params,
+        cost_estimate=pl.CostEstimate(flops=0, bytes_accessed=2 * back.size * 4, transcendentals=0),
+    )(back)
+    rcv_out = pl.pallas_call(
+        functools.partial(turn_rcv_kernel, own_rows),
+        in_specs=[pl.BlockSpec(memory_space=pltpu.SMEM), in_vmem, in_vmem],
+        out_shape=jax.ShapeDtypeStruct((RCV_DEV, bins), jnp.float32),
+        scratch_shapes=scratch,
+        compiler_params=params,
+    )(core, mine, other)
+    return shot_out, rcv_out
 
 
 def shards(traces, trace_shot, trace_rcv, fold_count):
@@ -371,8 +391,7 @@
     mine = parts[0][:, own_rows[0] : own_rows[0] + taken, :]
     counts = pair_counts(mine, lax.ppermute(mine, "shot", swap), lines, shot_blocks, rcv_blocks)
     back = exchange(solve(parts, counts, own_rows, shot_blocks, rcv_blocks))
-    other = lax.ppermute(back[:, owned:, :], "shot", swap)
-    return tuple(turn(core, back, other, own_rows))
+    return turn(core, back, swap, own_rows)
 
 
 def solution(mesh):

time: 83.8 us -> 83.5 us (level)
  waiting for transfers between devices: 15.8 us -> 14.9 us
    ppermute x1, waiting for transfers between devices: 1.52 us -> 0.52 us  [turn(): other = lax.ppermute(mine, 'shot', swap)]
    pallas_call x1 -> x2, Pallas kernels: 1.18 us -> 2.01 us  [the longest x1 1.01 us: turn(): pl.pallas_call(functools.partial(turn_rcv_kernel, own_rows), in_specs=[pl...]
  transfers between devices with their start and end apart: 5 -> 5, of which waited for: 5 -> 5; matrix products, arithmetic and copies ran while one was open for 2% -> 2% of each run, Pallas kernels for 18% -> 19%
where the time goes in v7:
time: 83.5 us; the launch traced here: 83 us
  Pallas kernels  27 us (32%)
  blocking collectives  24 us (29%)
  waiting for transfers between devices  14.9 us (18%)
  starting transfers between devices  11.8 us (14%)
  local copies, waits for them, and re-layouts  2.25 us (3%)
  other arithmetic  1.69 us (2%)
  between operations  1.35 us (2%)
    all_to_all x1, blocking collectives, shards(): back = exchange(solve(parts, counts, own_rows, shot_blocks, rcv_blocks))  24 us
    pallas_call x2, Pallas kernels, spectra_sums(): pl.pallas_call(functools.partial(spectra_kernel, places, 1.0 / samples, k...  18.1 us
    all_to_all x2, waiting for transfers between devices, shards(): parts.append(exchange(sums))  11.4 us
    all_to_all x2, starting transfers between devices, shards(): parts.append(exchange(sums))  11.3 us
    pallas_call x1, Pallas kernels, pair_counts(): pl.pallas_call(functools.partial(pairs_kernel, lines), out_shape=[jax.Sha...  4.19 us
    pallas_call x1, Pallas kernels, solve(): pl.pallas_call(functools.partial(solve_kernel, shot_blocks, rcv_blocks, o...  2.66 us
    unnamed x4, local copies, waits for them, and re-layouts  2.21 us
    scatter-add x1, other arithmetic, shards(): sums.at[:, sums.shape[1] - owned // 2:, :]  1.69 us
  transfers between devices with their start and end apart: 5, of which 5 were waited for; matrix products, arithmetic and copies ran while one was open for 2% of the time, Pallas kernels for 19%

profile of v7, /device:TPU:0, one launch (start us, length us, event | category | flops | bytes accessed | tf_op | source)
XLA Modules:
  0.0 83.0 jit_solution(11576258755975639773)
XLA Ops:
  1.3 7.3 %shard_map.95 = (f32[32,32,128]{2,1,0:T(8,128)}, f32[32,16,128]{2,1,0:T(8,128)}) custom-call(bf16[1536,2048]{1,0:T(8,128)(2,1)} %bitcast.4, bf16[1,512,512]{2,1,0:T(8,128)(2,1)} %constant.54.clone.refs_0_, bf16[1,512,512]{2,1,0:T(8,128)(2,1)} %constant.55.clone.refs_1_, s32[1,1536]{1,0:T(1,128)} %bitcast.6, s32[1,1536]{1,0:T(1,128)} %bitcast.8, ...), custom_call_target="tpu_custom_call" | custom-call | flops 1610612736 | bytes 7340032 | tf_op jit(solution)/shard_map/pallas_call | solution.py:180
  8.6 7.3 %all-to-all-start = ((f32[32,32,128]{2,1,0:T(8,128)}), f32[32,32,128]{2,1,0:T(8,128)S(1)}, u32[]{:S(2)}, u32[]{:S(2)}) async-start(f32[32,32,128]{2,1,0:T(8,128)} %get-tuple-element.22), calls=%async_computation | async-start | bytes 1048576 | tf_op jit(solution)/shard_map/all_to_all | solution.py:389
  15.9 10.8 %shard_map.96 = (f32[32,32,128]{2,1,0:T(8,128)}, f32[32,16,128]{2,1,0:T(8,128)}) custom-call(bf16[1536,2048]{1,0:T(8,128)(2,1)} %bitcast.5, bf16[1,512,1024]{2,1,0:T(8,128)(2,1)} %constant.56.clone.refs_0_, bf16[1,512,2048]{2,1,0:T(8,128)(2,1)} %constant.57.clone.refs_1_, s32[1,1536]{1,0:T(1,128)} %bitcast.7, s32[1,1536]{1,0:T(1,128)} %bitcast.9, ...), custom_call_target="tpu_custom_call" | custom-call | flops 4831838208 | bytes 9437184 | tf_op jit(solution)/shard_map/pallas_call | solution.py:180
  26.7 0.3 collective-permute-start
  27.0 1.5 %collective-permute-done = f32[32,16,128]{2,1,0:T(8,128)S(1)} collective-permute-done((f32[32,16,128]{2,1,0:T(8,128)}, f32[32,16,128]{2,1,0:T(8,128)S(1)}, u32[]{:S(2)}, u32[]{:S(2)}) %collective-permute-start) | collective-permute-done | bytes 262176 | tf_op jit(solution)/shard_map/ppermute | solution.py:388
  28.5 1.7 %add_dynamic-update-slice_fusion = f32[32,32,128]{2,1,0:T(8,128)} fusion(f32[32,32,128]{2,1,0:T(8,128)} %get-tuple-element.24, f32[32,16,128]{2,1,0:T(8,128)S(1)} %collective-permute-done), kind=kLoop, calls=%fused_computation | loop fusion | flops 65536 | bytes 786432 | tf_op jit(solution)/shard_map/scatter-add | solution.py:388
  30.2 2.0 %all-to-all-done.refs_0_ = f32[32,32,128]{2,1,0:T(8,128)S(1)} async-done(((f32[32,32,128]{2,1,0:T(8,128)}), f32[32,32,128]{2,1,0:T(8,128)S(1)}, u32[]{:S(2)}, u32[]{:S(2)}) %all-to-all-start) | async-done | bytes 524320 | tf_op jit(solution)/shard_map/all_to_all | solution.py:389
  32.3 4.0 %all-to-all-start.1 = ((f32[32,32,128]{2,1,0:T(8,128)}), f32[32,32,128]{2,1,0:T(8,128)S(1)}, u32[]{:S(2)}, u32[]{:S(2)}) async-start(f32[32,32,128]{2,1,0:T(8,128)} %add_dynamic-update-slice_fusion), calls=%async_computation.1 | async-start | bytes 1048576 | tf_op jit(solution)/shard_map/all_to_all | solution.py:389
  36.3 0.1 collective-permute-start.1
  36.4 1.5 %collective-permute-done.1.other_ref = f32[32,16,128]{2,1,0:T(8,128)S(1)} collective-permute-done((f32[32,16,128]{2,1,0:T(8,128)S(1)}, f32[32,16,128]{2,1,0:T(8,128)S(1)}, u32[]{:S(2)}, u32[]{:S(2)}) %collective-permute-start.1) | collective-permute-done | bytes 262176 | tf_op jit(solution)/shard_map/ppermute | solution.py:392
  37.9 4.2 %shard_map.97 = (bf16[512,1024]{1,0:T(8,128)(2,1)S(1)}, bf16[512,1024]{1,0:T(8,128)(2,1)S(1)}, f32[8,512]{1,0:T(8,128)S(1)}, f32[8,1024]{1,0:T(8,128)S(1)}) custom-call(f32[32,16,128]{2,1,0:T(8,128)S(1)} %slice.33.mine_ref, f32[32,16,128]{2,1,0:T(8,128)S(1)} %collective-permute-done.1.other_ref), custom_call_target="tpu_custom_call" | custom-call | flops 1610612736 | bytes 2097152 | tf_op jit(solution)/shard_map/pallas_call | solution.py:231
  42.1 0.0 copy-start
  42.1 1.0 %copy-done = bf16[512,1024]{1,0:T(8,128)(2,1)} copy-done((bf16[512,1024]{1,0:T(8,128)(2,1)}, bf16[512,1024]{1,0:T(8,128)(2,1)S(1)}, u32[]{:S(2)}) %copy-start) | copy-done | bytes 1048600
  43.1 9.4 %all-to-all-done.1.refs_1_ = f32[32,32,128]{2,1,0:T(8,128)S(1)} async-done(((f32[32,32,128]{2,1,0:T(8,128)}), f32[32,32,128]{2,1,0:T(8,128)S(1)}, u32[]{:S(2)}, u32[]{:S(2)}) %all-to-all-start.1) | async-done | bytes 524320 | tf_op jit(solution)/shard_map/all_to_all | solution.py:389
  52.4 0.0 copy-start.1
  52.4 1.2 %copy-done.1 = bf16[512,1024]{1,0:T(8,128)(2,1)S(1)} copy-done((bf16[512,1024]{1,0:T(8,128)(2,1)S(1)}, bf16[512,1024]{1,0:T(8,128)(2,1)}, u32[]{:S(2)}) %copy-start.1) | copy-done | bytes 1048600
  53.7 2.7 %shard_map.98 = f32[32,48,128]{2,1,0:T(8,128)S(1)} custom-call(f32[32,32,128]{2,1,0:T(8,128)S(1)} %all-to-all-done.refs_0_, f32[32,32,128]{2,1,0:T(8,128)S(1)} %all-to-all-done.1.refs_1_, bf16[512,1024]{1,0:T(8,128)(2,1)S(1)} %get-tuple-element.26.refs_2_, bf16[512,1024]{1,0:T(8,128)(2,1)S(1)} %copy-done.1, f32[8,512]{1,0:T(8,128)S(1)} %get-tuple-element.28.refs_4_, ...), custom_call_target="tpu_custom_call" | custom-call | tf_op jit(solution)/shard_map/pallas_call | solution.py:294
  56.3 24.0 %all_to_all.15.back = f32[32,48,128]{2,1,0:T(8,128)S(1)} all-to-all(f32[32,48,128]{2,1,0:T(8,128)S(1)} %shard_map.98), channel_id=1, replica_groups=mesh['shot'=4,'rcv'=8] {'shot','rcv'}, dimensions={0} | all-to-all | bytes 1572864 | tf_op jit(solution)/shard_map/all_to_all | solution.py:393
  80.4 0.1 collective-permute-start.2
  80.5 1.0 %shard_map.99 = f32[128,1024]{1,0:T(8,128)} custom-call(f32[32,48,128]{2,1,0:T(8,128)S(1)} %all_to_all.15.back), custom_call_target="tpu_custom_call" | custom-call | bytes 1572864 | tf_op jit(solution)/shard_map/pallas_call | solution.py:331
  81.5 0.5 collective-permute-done.2.other
  82.0 1.0 %shard_map.100 = f32[128,1024]{1,0:T(8,128)} custom-call(s32[1]{0:T(128)} %bitcast.3.refs_5_.core_ref, f32[32,16,128]{2,1,0:T(8,128)S(1)} %slice.34.mine, f32[32,16,128]{2,1,0:T(8,128)S(1)} %collective-permute-done.2.other), custom_call_target="tpu_custom_call" | custom-call | tf_op jit(solution)/shard_map/pallas_call | solution.py:339
  (2 shorter events, 0.0 us)
Async XLA Ops:
  8.6 23.7 %all-to-all-start = ((f32[32,32,128]{2,1,0:T(8,128)}), f32[32,32,128]{2,1,0:T(8,128)S(1)}, u32[]{:S(2)}, u32[]{:S(2)}) async-start(f32[32,32,128]{2,1,0:T(8,128)} %get-tuple-element.22), calls=%async_computation | async-start | bytes 1048576 | tf_op jit(solution)/shard_map/all_to_all | solution.py:389
  26.7 1.8 %collective-permute-start = (f32[32,16,128]{2,1,0:T(8,128)}, f32[32,16,128]{2,1,0:T(8,128)S(1)}, u32[]{:S(2)}, u32[]{:S(2)}) collective-permute-start(f32[32,16,128]{2,1,0:T(8,128)} %get-tuple-element.25), channel_id=1, source_target_pairs={{0,8},{8,0},{16,24},{24,16},{1,9},{9,1},{17,25},{25,17},{2,10},{10... | collective-permute-start | bytes 786440 | tf_op jit(solution)/shard_map/ppermute | solution.py:388
  32.3 20.2 %all-to-all-start.1 = ((f32[32,32,128]{2,1,0:T(8,128)}), f32[32,32,128]{2,1,0:T(8,128)S(1)}, u32[]{:S(2)}, u32[]{:S(2)}) async-start(f32[32,32,128]{2,1,0:T(8,128)} %add_dynamic-update-slice_fusion), calls=%async_computation.1 | async-start | bytes 1048576 | tf_op jit(solution)/shard_map/all_to_all | solution.py:389
  36.3 1.6 %collective-permute-start.1 = (f32[32,16,128]{2,1,0:T(8,128)S(1)}, f32[32,16,128]{2,1,0:T(8,128)S(1)}, u32[]{:S(2)}, u32[]{:S(2)}) collective-permute-start(f32[32,16,128]{2,1,0:T(8,128)S(1)} %slice.33.mine_ref), channel_id=1, source_target_pairs={{0,8},{8,0},{16,24},{24,16},{1,9},{9,1},{17,25},{25,17},{2,10},{10... | collective-permute-start | bytes 786440 | tf_op jit(solution)/shard_map/ppermute | solution.py:392
  42.1 1.0 %copy-start = (bf16[512,1024]{1,0:T(8,128)(2,1)}, bf16[512,1024]{1,0:T(8,128)(2,1)S(1)}, u32[]{:S(2)}) copy-start(bf16[512,1024]{1,0:T(8,128)(2,1)S(1)} %get-tuple-element.27.refs_3_) | copy-start | bytes 3145732
  52.4 1.2 %copy-start.1 = (bf16[512,1024]{1,0:T(8,128)(2,1)S(1)}, bf16[512,1024]{1,0:T(8,128)(2,1)}, u32[]{:S(2)}) copy-start(bf16[512,1024]{1,0:T(8,128)(2,1)} %copy-done) | copy-start | bytes 3145732
  80.4 1.6 %collective-permute-start.2 = (f32[32,16,128]{2,1,0:T(8,128)S(1)}, f32[32,16,128]{2,1,0:T(8,128)S(1)}, u32[]{:S(2)}, u32[]{:S(2)}) collective-permute-start(f32[32,16,128]{2,1,0:T(8,128)S(1)} %slice.34.mine), channel_id=1, source_target_pairs={{0,8},{8,0},{16,24},{24,16},{1,9},{9,1},{17,25},{25,17},{2,10},{10... | collective-permute-start | bytes 786440 | tf_op jit(solution)/shard_map/ppermute | solution.py:330
